TPU v7x, 128 devices: a whole 4x4x4 slice. The times are simulated.
128 devices in a mesh: wide: 16 (over y, z_hi, core), narrow: 8 (over x, z_lo).
Axes of the slice: x: 4, y: 4, z: 4 (z_hi: 2, z_lo: 2; z = z_hi * 2 + z_lo), core: 2. Of those that a mesh axis runs over, the one named last changes fastest.
Arguments:
- node_hidden_state: bfloat16 [262144, 128], P(('wide', 'narrow')), may hold values from -6 to 6
- edge_hidden_state: bfloat16 [1572864, 128], P(('wide', 'narrow')), may hold values from -6 to 6
- node_output_gradient: bfloat16 [262144, 128], P(('wide', 'narrow')), may hold values from -6 to 6
- edge_output_gradient: bfloat16 [1572864, 128], P(('wide', 'narrow')), may hold values from -6 to 6
- senders: int32 [1572864], P(('wide', 'narrow')), may hold values from 0 to 4095
- receivers: int32 [1572864], P(('wide', 'narrow')), may hold values from 0 to 2047, as said below
- edge_slot_count: int32 [128], P(('wide', 'narrow')), may hold values from 3072 to 12288, as said below
- outbound_rows: int32 [128, 4, 512], P(('wide', 'narrow')), may hold values from 0 to 2047, as said below
- edge_weight_in: bfloat16 [384, 128], replicated, may hold values from -0.3125 to 0.3125
- edge_weight_mid: bfloat16 [128, 128], replicated, may hold values from -0.5 to 0.5
- edge_weight_out: bfloat16 [128, 128], replicated, may hold values from -0.5 to 0.5
- node_weight_in: bfloat16 [256, 128], replicated, may hold values from -0.375 to 0.375
- node_weight_mid: bfloat16 [128, 128], replicated, may hold values from -0.5 to 0.5
- node_weight_out: bfloat16 [128, 128], replicated, may hold values from -0.5 to 0.5
Outputs:
- node_state_gradient: float32 [262144, 128], P(('wide', 'narrow'))
- edge_grad: bfloat16 [1572864, 128], P(('wide', 'narrow'))
- edge_in_grad: float32 [384, 128], replicated
- edge_mid_grad: float32 [128, 128], replicated
- edge_out_grad: float32 [128, 128], replicated
- node_in_grad: float32 [256, 128], replicated
- node_mid_grad: float32 [128, 128], replicated
- node_out_grad: float32 [128, 128], replicated
Inputs may be any that keep to these rules, and one draw needn't show every extreme that they name: `receivers`: Non-decreasing within each partition's 12288 slots. `edge_slot_count`: some partition is full in every draw. `outbound_rows`: the 512 rows of one list are distinct.
All inputs are finite; a program needn't handle non-finite values.
Results may differ from a plain program's by a relative error of at most 0.015.
Values may be sent and summed in bfloat16 or wider, within the bound.
A program may use at most 128 MiB of HBM per device.

v0:
```python
import math

import jax
import jax.numpy as jnp
from jax import lax
from jax.sharding import PartitionSpec as P

BLOCK = 2048


epsilon = 1e-05


def extended_2(shard, sides, width):
    for axis, dim in sides:
        size, length = (lax.axis_size(axis), shard.shape[dim])
        up = [(i, (i + 1) % size) for i in range(size - 1)]
        down = [(j, i) for i, j in up]
        last = lax.slice_in_dim(shard, length - width, length, axis=dim)
        leading = lax.slice_in_dim(shard, 0, width, axis=dim)
        before = lax.ppermute(last, axis, up)
        after = lax.ppermute(leading, axis, down)
        shard = jnp.concatenate([before, shard, after], axis=dim)
    return shard


def silu_slope(values):
    sigmoid = jax.nn.sigmoid(values)
    return sigmoid * (1.0 + values * (1.0 - sigmoid))


def mlp_forward(inputs, weight_in, weight_mid, weight_out):
    first_pre = jnp.dot(inputs, weight_in, preferred_element_type=jnp.float32)
    first_act = jax.nn.silu(first_pre).astype(jnp.bfloat16)
    second_pre = jnp.dot(first_act, weight_mid, preferred_element_type=jnp.float32)
    second_act = jax.nn.silu(second_pre).astype(jnp.bfloat16)
    top_pre = jnp.dot(second_act, weight_out, preferred_element_type=jnp.float32)
    centred = top_pre - jnp.mean(top_pre, axis=-1, keepdims=True)
    inverse = lax.rsqrt(jnp.mean(centred * centred, axis=-1, keepdims=True) + epsilon)
    normed = centred * inverse
    return (normed, (first_pre, first_act, second_pre, second_act, normed, inverse))


def mlp_backward(inputs, stored, upstream, weight_in, weight_mid, weight_out):
    first_pre, first_act, second_pre, second_act, normed, inverse = stored
    top_grad = inverse * (
        upstream
        - jnp.mean(upstream, axis=-1, keepdims=True)
        - normed * jnp.mean(upstream * normed, axis=-1, keepdims=True)
    )
    top_grad = top_grad.astype(jnp.bfloat16)
    out_wgrad = jnp.dot(second_act.T, top_grad, preferred_element_type=jnp.float32)
    second_grad = jnp.dot(top_grad, weight_out.T, preferred_element_type=jnp.float32)
    second_grad = (second_grad * silu_slope(second_pre)).astype(jnp.bfloat16)
    mid_wgrad = jnp.dot(first_act.T, second_grad, preferred_element_type=jnp.float32)
    first_grad = jnp.dot(second_grad, weight_mid.T, preferred_element_type=jnp.float32)
    first_grad = (first_grad * silu_slope(first_pre)).astype(jnp.bfloat16)
    in_wgrad = jnp.dot(inputs.T, first_grad, preferred_element_type=jnp.float32)
    input_grad = jnp.dot(first_grad, weight_in.T, preferred_element_type=jnp.float32)
    return (input_grad, (in_wgrad, mid_wgrad, out_wgrad))


def per_device(
    node_hidden_state,
    edge_hidden_state,
    node_output_gradient,
    edge_output_gradient,
    senders,
    receivers,
    edge_slot_count,
    outbound_rows,
    edge_weight_in,
    edge_weight_mid,
    edge_weight_out,
    node_weight_in,
    node_weight_mid,
    node_weight_out,
):
    features = node_hidden_state.shape[1]
    node_rows = node_hidden_state.shape[0]
    edge_rows = edge_hidden_state.shape[0]
    halo_rows = outbound_rows.shape[2]
    partitions = lax.axis_size("wide") * lax.axis_size("narrow")
    send_ids = outbound_rows[0].reshape(4 * halo_rows)
    outgoing = node_hidden_state[send_ids].reshape(4, halo_rows, features)
    wide_in = extended_2(outgoing[0:2], (("wide", 0),), 1)
    narrow_in = extended_2(outgoing[2:4], (("narrow", 0),), 1)
    extended = jnp.concatenate(
        [node_hidden_state, wide_in[0], wide_in[3], narrow_in[0], narrow_in[3]], 0
    )
    live_count = edge_slot_count[0]
    blocks = edge_rows // BLOCK
    offsets = jnp.arange(blocks, dtype=jnp.int32) * BLOCK
    latent_blocks = edge_hidden_state.reshape(blocks, BLOCK, features)
    sender_blocks = senders.reshape(blocks, BLOCK)
    receiver_blocks = receivers.reshape(blocks, BLOCK)
    cotangent_blocks = edge_output_gradient.reshape(blocks, BLOCK, features)

    def inputs_of(latent_block, sender_block, receiver_block):
        return jnp.concatenate(
            [latent_block, extended[sender_block], node_hidden_state[receiver_block]], 1
        )

    def live_of(offset):
        return (offset + jnp.arange(BLOCK, dtype=jnp.int32) < live_count)[:, None]

    def forward_step(aggregate, call_arguments):
        latent_block, sender_block, receiver_block, offset = call_arguments
        edge_out, stored = mlp_forward(
            inputs_of(latent_block, sender_block, receiver_block),
            edge_weight_in,
            edge_weight_mid,
            edge_weight_out,
        )
        message = jnp.where(live_of(offset), edge_out, 0.0).astype(jnp.bfloat16)
        message = lax.optimization_barrier(message).astype(jnp.float32)
        added = jax.ops.segment_sum(
            message, receiver_block, num_segments=node_rows, indices_are_sorted=True
        )
        return (aggregate + added, None)

    aggregate, kept = lax.scan(
        forward_step,
        jnp.zeros((node_rows, features), jnp.float32),
        (latent_blocks, sender_blocks, receiver_blocks, offsets),
    )
    aggregate = aggregate.astype(jnp.bfloat16)
    node_inputs = jnp.concatenate([node_hidden_state, aggregate], 1)
    node_stored = mlp_forward(node_inputs, node_weight_in, node_weight_mid, node_weight_out)[1]
    node_input_grad, node_wgrads = mlp_backward(
        node_inputs,
        node_stored,
        node_output_gradient.astype(jnp.float32),
        node_weight_in,
        node_weight_mid,
        node_weight_out,
    )
    node_sums = node_wgrads
    aggregate_grad = node_input_grad[:, features:]
    initial_grad = jnp.concatenate(
        [
            node_output_gradient.astype(jnp.float32) + node_input_grad[:, :features],
            jnp.zeros((4 * halo_rows, features), jnp.float32),
        ],
        0,
    )
    initial_wgrads = (
        jnp.zeros(edge_weight_in.shape, jnp.float32),
        jnp.zeros(edge_weight_mid.shape, jnp.float32),
        jnp.zeros(edge_weight_out.shape, jnp.float32),
    )

    def backward_core(
        carried, latent_block, sender_block, receiver_block, cotangent_block, offset, stored
    ):
        widened_gradient, wgrads = carried
        inputs = inputs_of(latent_block, sender_block, receiver_block)
        live_mask = live_of(offset)
        cotangent = cotangent_block.astype(jnp.float32)
        upstream = jnp.where(live_mask, cotangent + aggregate_grad[receiver_block], 0.0)
        input_grad, block_wgrads = mlp_backward(
            inputs, stored, upstream, edge_weight_in, edge_weight_mid, edge_weight_out
        )
        block_grad = jnp.where(live_mask, cotangent + input_grad[:, :features], 0.0).astype(
            jnp.bfloat16
        )
        widened_gradient = widened_gradient.at[sender_block].add(
            input_grad[:, features : 2 * features]
        )
        widened_gradient = widened_gradient.at[receiver_block].add(input_grad[:, 2 * features :])
        wgrads = jax.tree.map(lambda total, added: total + added, wgrads, block_wgrads)
        return ((widened_gradient, wgrads), block_grad)

    def backward_step(carried, call_arguments):
        latent_block, sender_block, receiver_block, cotangent_block, offset = call_arguments
        stored = mlp_forward(
            inputs_of(latent_block, sender_block, receiver_block),
            edge_weight_in,
            edge_weight_mid,
            edge_weight_out,
        )[1]
        return backward_core(
            carried, latent_block, sender_block, receiver_block, cotangent_block, offset, stored
        )

    scanned = (latent_blocks, sender_blocks, receiver_blocks, cotangent_blocks, offsets)
    (widened_gradient, edge_wgrads), grad_blocks = lax.scan(
        backward_step, (initial_grad, initial_wgrads), scanned
    )
    edge_grad = grad_blocks.reshape(edge_rows, features)
    border_gradient = widened_gradient[node_rows:].reshape(4, halo_rows, features)
    wide_back = extended_2(border_gradient[0:2].astype(jnp.bfloat16), (("wide", 0),), 1).astype(
        jnp.float32
    )
    narrow_back = extended_2(border_gradient[2:4].astype(jnp.bfloat16), (("narrow", 0),), 1).astype(
        jnp.float32
    )
    results_back = jnp.concatenate([wide_back[0], wide_back[3], narrow_back[0], narrow_back[3]], 0)
    node_state_gradient = widened_gradient[:node_rows].at[send_ids].add(results_back)
    summed = lax.psum(
        (edge_wgrads[0], edge_wgrads[1], edge_wgrads[2], node_sums[0], node_sums[1], node_sums[2]),
        ("wide", "narrow"),
    )
    edge_sums = summed[0:3]
    node_sums = summed[3:6]
    edge_scale = 1.0 / math.sqrt(edge_rows * partitions)
    node_scale = 1.0 / math.sqrt(node_rows * partitions)
    return (
        node_state_gradient,
        edge_grad,
        edge_sums[0] * edge_scale,
        edge_sums[1] * edge_scale,
        edge_sums[2] * edge_scale,
        node_sums[0] * node_scale,
        node_sums[1] * node_scale,
        node_sums[2] * node_scale,
    )


def solution(mesh):
    placed = (
        P(("wide", "narrow"), None),
        P(("wide", "narrow"), None),
        P(("wide", "narrow"), None),
        P(("wide", "narrow"), None),
        P(("wide", "narrow")),
        P(("wide", "narrow")),
        P(("wide", "narrow")),
        P(("wide", "narrow"), None, None),
        P(),
        P(),
        P(),
        P(),
        P(),
        P(),
    )
    return jax.shard_map(
        per_device,
        mesh=mesh,
        in_specs=placed,
        out_specs=(
            P(("wide", "narrow"), None),
            P(("wide", "narrow"), None),
            P(),
            P(),
            P(),
            P(),
            P(),
            P(),
        ),
        check_vma=False,
    )
```

profile of v0, /device:TPU:32, one launch (start us, length us, event | category | flops | bytes accessed | tf_op | source)
XLA Modules:
  0.0 974.5 jit_solution(7279045638368739924)
XLA Ops:
  8.0 6.8 gather_fusion.5
  16.9 4.8 collective-permute-start.2
  23.1 3.2 collective-permute-start
  29.7 236.1 %while.29 = (s32[]{:T(128)}, f32[2048,128]{1,0:T(8,128)S(1)}, s32[6,2048]{1,0:T(8,128)}, s32[6]{0:T(128)S(1)}, s32[]{:T(128)}, /*index=5*/bf16[6,2048,128]{2,1,0...) while((s32[]{:T(128)}, f32[2048,128]{1,0:T(8,128)S(1)}, ...), condition=%wide.region_4.5_spmd, body=%wide.region_0.4_spmd.sunk | while | flops 345266176 | bytes 14495905 | solution.py:122
  32.5 6.2 gather_fusion.1
  38.7 8.1 gather_fusion
  48.6 2.9 multiply_convert_fusion.11
  54.4 12.2 %scatter_fusion = f32[2048,128]{1,0:T(8,128)S(1)} fusion(f32[2048,128]{1,0:T(8,128)S(1)} %get-tuple-element.601, s32[2048]{0:T(1024)S(1)} %bitcast.187, f32[2048,128]{1,0:T(8,128)} %copy.48), kind=kCustom, calls=%fused_computation.6.clone.1 | custom fusion | flops 262144 | bytes 3153920 | tf_op jit(solution)/shard_map/while/body/eval_jaxpr/scatter-add | solution.py:117
  69.5 6.2 gather_fusion.1
  75.7 8.1 gather_fusion
  85.6 2.9 multiply_convert_fusion.11
  91.4 13.5 %scatter_fusion = f32[2048,128]{1,0:T(8,128)S(1)} fusion(f32[2048,128]{1,0:T(8,128)S(1)} %get-tuple-element.601, s32[2048]{0:T(1024)S(1)} %bitcast.187, f32[2048,128]{1,0:T(8,128)} %copy.48), kind=kCustom, calls=%fused_computation.6.clone.1 | custom fusion | flops 262144 | bytes 3153920 | tf_op jit(solution)/shard_map/while/body/eval_jaxpr/scatter-add | solution.py:117
  107.8 6.2 gather_fusion.1
  114.0 8.1 gather_fusion
  123.9 2.9 multiply_convert_fusion.11
  129.7 15.5 %scatter_fusion = f32[2048,128]{1,0:T(8,128)S(1)} fusion(f32[2048,128]{1,0:T(8,128)S(1)} %get-tuple-element.601, s32[2048]{0:T(1024)S(1)} %bitcast.187, f32[2048,128]{1,0:T(8,128)} %copy.48), kind=kCustom, calls=%fused_computation.6.clone.1 | custom fusion | flops 262144 | bytes 3153920 | tf_op jit(solution)/shard_map/while/body/eval_jaxpr/scatter-add | solution.py:117
  148.0 6.2 gather_fusion.1
  154.2 8.1 gather_fusion
  164.1 2.9 multiply_convert_fusion.11
  169.9 15.5 %scatter_fusion = f32[2048,128]{1,0:T(8,128)S(1)} fusion(f32[2048,128]{1,0:T(8,128)S(1)} %get-tuple-element.601, s32[2048]{0:T(1024)S(1)} %bitcast.187, f32[2048,128]{1,0:T(8,128)} %copy.48), kind=kCustom, calls=%fused_computation.6.clone.1 | custom fusion | flops 262144 | bytes 3153920 | tf_op jit(solution)/shard_map/while/body/eval_jaxpr/scatter-add | solution.py:117
  188.2 6.2 gather_fusion.1
  194.4 8.1 gather_fusion
  204.3 2.9 multiply_convert_fusion.11
  210.1 15.5 %scatter_fusion = f32[2048,128]{1,0:T(8,128)S(1)} fusion(f32[2048,128]{1,0:T(8,128)S(1)} %get-tuple-element.601, s32[2048]{0:T(1024)S(1)} %bitcast.187, f32[2048,128]{1,0:T(8,128)} %copy.48), kind=kCustom, calls=%fused_computation.6.clone.1 | custom fusion | flops 262144 | bytes 3153920 | tf_op jit(solution)/shard_map/while/body/eval_jaxpr/scatter-add | solution.py:117
  228.4 6.2 gather_fusion.1
  234.6 8.1 gather_fusion
  244.5 2.9 multiply_convert_fusion.11
  250.3 15.5 %scatter_fusion = f32[2048,128]{1,0:T(8,128)S(1)} fusion(f32[2048,128]{1,0:T(8,128)S(1)} %get-tuple-element.601, s32[2048]{0:T(1024)S(1)} %bitcast.187, f32[2048,128]{1,0:T(8,128)} %copy.48), kind=kCustom, calls=%fused_computation.6.clone.1 | custom fusion | flops 262144 | bytes 3153920 | tf_op jit(solution)/shard_map/while/body/eval_jaxpr/scatter-add | solution.py:117
  281.6 2.7 concatenate.27.clone
  284.3 506.0 %while.30 = (s32[]{:T(128)}, f32[4096,128]{1,0:T(8,128)}, f32[384,128]{1,0:T(8,128)}, f32[128,128]{1,0:T(8,128)S(1)}, f32[128,128]{1,0:T(8,128)S(1)}, /*index=5*...) while((s32[]{:T(128)}, f32[4096,128]{1,0:T(8,128)}, ...), condition=%wide.region_16.17_spmd.clone, body=%wide.region_9.16_spmd.clone.sunk | while | flops 1030940672 | bytes 75694504 | solution.py:187
  287.2 8.0 gather_fusion.3
  295.1 8.0 gather_fusion.2
  308.1 7.6 gather_fusion.4
  329.9 2.6 copy.51
  335.9 14.8 %scatter_custom_fusion.17 = f32[4096,128]{1,0:T(8,128)} fusion(f32[4096,128]{1,0:T(8,128)} %get-tuple-element.647, s32[2048]{0:T(1024)S(1)} %bitcast.189, f32[2048,384]{1,0:T(8,128)} %copy-done.2), kind=kCustom, calls=%fused_computation.48.clone.1 | custom fusion | flops 262144 | bytes 3145728 | tf_op jit(solution)/shard_map/while/body/eval_jaxpr/scatter-add | solution.py:167
  350.7 14.8 %scatter_custom_fusion.18 = f32[4096,128]{1,0:T(8,128)} fusion(f32[4096,128]{1,0:T(8,128)} %scatter_custom_fusion.17, s32[2048]{0:T(1024)S(1)} %bitcast.193, f32[2048,384]{1,0:T(8,128)} %copy-done.2), kind=kCustom, calls=%fused_computation.46.clone.1 | custom fusion | flops 262144 | bytes 3145728 | tf_op jit(solution)/shard_map/while/body/eval_jaxpr/scatter-add | solution.py:170
  369.1 8.0 gather_fusion.3
  377.1 8.0 gather_fusion.2
  390.1 7.6 gather_fusion.4
  417.9 14.8 %scatter_custom_fusion.17 = f32[4096,128]{1,0:T(8,128)} fusion(f32[4096,128]{1,0:T(8,128)} %get-tuple-element.647, s32[2048]{0:T(1024)S(1)} %bitcast.189, f32[2048,384]{1,0:T(8,128)} %copy-done.2), kind=kCustom, calls=%fused_computation.48.clone.1 | custom fusion | flops 262144 | bytes 3145728 | tf_op jit(solution)/shard_map/while/body/eval_jaxpr/scatter-add | solution.py:167
  432.6 16.1 %scatter_custom_fusion.18 = f32[4096,128]{1,0:T(8,128)} fusion(f32[4096,128]{1,0:T(8,128)} %scatter_custom_fusion.17, s32[2048]{0:T(1024)S(1)} %bitcast.193, f32[2048,384]{1,0:T(8,128)} %copy-done.2), kind=kCustom, calls=%fused_computation.46.clone.1 | custom fusion | flops 262144 | bytes 3145728 | tf_op jit(solution)/shard_map/while/body/eval_jaxpr/scatter-add | solution.py:170
  452.4 8.0 gather_fusion.3
  460.4 8.0 gather_fusion.2
  473.3 7.6 gather_fusion.4
  501.1 14.8 %scatter_custom_fusion.17 = f32[4096,128]{1,0:T(8,128)} fusion(f32[4096,128]{1,0:T(8,128)} %get-tuple-element.647, s32[2048]{0:T(1024)S(1)} %bitcast.189, f32[2048,384]{1,0:T(8,128)} %copy-done.2), kind=kCustom, calls=%fused_computation.48.clone.1 | custom fusion | flops 262144 | bytes 3145728 | tf_op jit(solution)/shard_map/while/body/eval_jaxpr/scatter-add | solution.py:167
  515.9 18.0 %scatter_custom_fusion.18 = f32[4096,128]{1,0:T(8,128)} fusion(f32[4096,128]{1,0:T(8,128)} %scatter_custom_fusion.17, s32[2048]{0:T(1024)S(1)} %bitcast.193, f32[2048,384]{1,0:T(8,128)} %copy-done.2), kind=kCustom, calls=%fused_computation.46.clone.1 | custom fusion | flops 262144 | bytes 3145728 | tf_op jit(solution)/shard_map/while/body/eval_jaxpr/scatter-add | solution.py:170
  537.6 8.0 gather_fusion.3
  545.6 8.0 gather_fusion.2
  558.5 7.6 gather_fusion.4
  586.3 14.8 %scatter_custom_fusion.17 = f32[4096,128]{1,0:T(8,128)} fusion(f32[4096,128]{1,0:T(8,128)} %get-tuple-element.647, s32[2048]{0:T(1024)S(1)} %bitcast.189, f32[2048,384]{1,0:T(8,128)} %copy-done.2), kind=kCustom, calls=%fused_computation.48.clone.1 | custom fusion | flops 262144 | bytes 3145728 | tf_op jit(solution)/shard_map/while/body/eval_jaxpr/scatter-add | solution.py:167
  601.1 18.0 %scatter_custom_fusion.18 = f32[4096,128]{1,0:T(8,128)} fusion(f32[4096,128]{1,0:T(8,128)} %scatter_custom_fusion.17, s32[2048]{0:T(1024)S(1)} %bitcast.193, f32[2048,384]{1,0:T(8,128)} %copy-done.2), kind=kCustom, calls=%fused_computation.46.clone.1 | custom fusion | flops 262144 | bytes 3145728 | tf_op jit(solution)/shard_map/while/body/eval_jaxpr/scatter-add | solution.py:170
  622.8 8.0 gather_fusion.3
  630.8 8.0 gather_fusion.2
  643.7 7.6 gather_fusion.4
  671.5 14.8 %scatter_custom_fusion.17 = f32[4096,128]{1,0:T(8,128)} fusion(f32[4096,128]{1,0:T(8,128)} %get-tuple-element.647, s32[2048]{0:T(1024)S(1)} %bitcast.189, f32[2048,384]{1,0:T(8,128)} %copy-done.2), kind=kCustom, calls=%fused_computation.48.clone.1 | custom fusion | flops 262144 | bytes 3145728 | tf_op jit(solution)/shard_map/while/body/eval_jaxpr/scatter-add | solution.py:167
  686.3 18.0 %scatter_custom_fusion.18 = f32[4096,128]{1,0:T(8,128)} fusion(f32[4096,128]{1,0:T(8,128)} %scatter_custom_fusion.17, s32[2048]{0:T(1024)S(1)} %bitcast.193, f32[2048,384]{1,0:T(8,128)} %copy-done.2), kind=kCustom, calls=%fused_computation.46.clone.1 | custom fusion | flops 262144 | bytes 3145728 | tf_op jit(solution)/shard_map/while/body/eval_jaxpr/scatter-add | solution.py:170
  708.0 8.0 gather_fusion.3
  716.0 8.0 gather_fusion.2
  728.9 7.6 gather_fusion.4
  756.7 14.8 %scatter_custom_fusion.17 = f32[4096,128]{1,0:T(8,128)} fusion(f32[4096,128]{1,0:T(8,128)} %get-tuple-element.647, s32[2048]{0:T(1024)S(1)} %bitcast.189, f32[2048,384]{1,0:T(8,128)} %copy-done.2), kind=kCustom, calls=%fused_computation.48.clone.1 | custom fusion | flops 262144 | bytes 3145728 | tf_op jit(solution)/shard_map/while/body/eval_jaxpr/scatter-add | solution.py:167
  771.5 18.0 %scatter_custom_fusion.18 = f32[4096,128]{1,0:T(8,128)} fusion(f32[4096,128]{1,0:T(8,128)} %scatter_custom_fusion.17, s32[2048]{0:T(1024)S(1)} %bitcast.193, f32[2048,384]{1,0:T(8,128)} %copy-done.2), kind=kCustom, calls=%fused_computation.46.clone.1 | custom fusion | flops 262144 | bytes 3145728 | tf_op jit(solution)/shard_map/while/body/eval_jaxpr/scatter-add | solution.py:170
  796.0 4.8 collective-permute-start.6
  805.2 12.4 %scatter_custom_fusion.3 = f32[2048,128]{1,0:T(8,128)S(1)} fusion(f32[2048,128]{1,0:T(8,128)S(1)} %slice.113, s32[2048]{0:T(1024)} %bitcast.195, f32[512,128]{1,0:T(8,128)S(1)} %get-tuple-element.360, f32[]{:T(128)} %constant.95, f32[512,128]{1,0:T(8,128)S(1)} %get-tuple-element.359, f32[512,128]{1,0:T(8,128)S(1)} %get-tuple-element.358, ...), kind=kCustom, calls=%fused_computation.88 | custom fusion | flops 1048576 | bytes 2097664 | tf_op jit(solution)/shard_map/scatter-add | solution.py:199
  817.6 141.0 %all-reduce.4.cloned.1.call-done = (f32[384,128]{1,0:T(8,128)}, f32[128,128]{1,0:T(8,128)}, f32[128,128]{1,0:T(8,128)}, f32[256,128]{1,0:T(8,128)}, f32[128,128]{1,0:T(8,128)}, /*index=5*/f32[128,128]{1,0:T(8,128)}) async-done(((f32[384,128]{1,0:T(8,128)}, f32[128,128]{1,0:T(8,128)}, f32[128,128]{1,0:T(8,128)}, f32[256,128]{1,0:T(8,128)}, f32[128,128]{1,0:T(8,128)}, /*index=5*/f32[128,128]{1,0:T(8,128)}), ...) | async-done | bytes 589840 | tf_op jit(solution)/shard_map/psum | solution.py:200
  (428 shorter events, 256.3 us)
Async XLA Ops:
  7.2 258.7 %copy-start = (bf16[256,128]{1,0:T(8,128)(2,1)S(1)}, bf16[256,128]{1,0:T(8,128)(2,1)}, u32[]{:S(2)}) copy-start(bf16[256,128]{1,0:T(8,128)(2,1)} %param.29) | copy-start | bytes 196612
  7.2 951.4 %all-reduce.4.cloned.1.call-start = ((), (), s32[]{:S(2)}) async-start(), calls=%async_computation | async-start | bytes 1179648 | tf_op jit(solution)/shard_map/psum | solution.py:200
  8.0 6.8 copy-start.18
  8.0 18.3 %copy-start.1 = (bf16[2048,128]{1,0:T(8,128)(2,1)S(1)}, bf16[2048,128]{1,0:T(8,128)(2,1)}, u32[]{:S(2)}) copy-start(bf16[2048,128]{1,0:T(8,128)(2,1)} %param.18) | copy-start | bytes 1572868
  14.8 11.6 %copy-start.16 = (s32[12288]{0:T(1024)S(1)}, s32[12288]{0:T(1024)}, u32[]{:S(2)}) copy-start(s32[12288]{0:T(1024)} %param.22) | copy-start | bytes 147460
  14.8 13.6 %copy-start.13 = (bf16[2048,128]{1,0:T(8,128)(2,1)S(1)}, bf16[2048,128]{1,0:T(8,128)(2,1)}, u32[]{:S(2)}) copy-start(bf16[2048,128]{1,0:T(8,128)(2,1)} %param.20) | copy-start | bytes 1572868
  14.8 14.7 %collective-permute-start.3 = (bf16[1,512,128]{2,1,0:T(8,128)(2,1)S(1)}, bf16[1,512,128]{2,1,0:T(8,128)(2,1)S(1)}, u32[]{:S(2)}, u32[]{:S(2)}) collective-permute-start(bf16[1,512,128]{2,1,0:T(8,128)(2,1)S(1)} %get-tuple-element.361), channel_id=1, source_target_pairs={{1,0},{2,1},{3,2},{4,3},{5,4},{6,5},{7,6},{9,8},{10,9},{11,10},{12... | collective-permute-start | bytes 393224 | tf_op jit(solution)/shard_map/ppermute | solution.py:22
  16.9 12.6 %collective-permute-start.2 = (bf16[1,512,128]{2,1,0:T(8,128)(2,1)S(1)}, bf16[1,512,128]{2,1,0:T(8,128)(2,1)S(1)}, u32[]{:S(2)}, u32[]{:S(2)}) collective-permute-start(bf16[1,512,128]{2,1,0:T(8,128)(2,1)S(1)} %get-tuple-element.362), channel_id=1, source_target_pairs={{0,1},{1,2},{2,3},{3,4},{4,5},{5,6},{6,7},{8,9},{9,10},{10,11},{11... | collective-permute-start | bytes 393224 | tf_op jit(solution)/shard_map/ppermute | solution.py:21
  21.7 7.7 collective-permute-start.1
  23.0 6.6 copy-start.8
  23.0 6.6 copy-start.9
  23.1 6.6 copy-start.20
  23.1 6.4 collective-permute-start
  265.9 0.8 copy-start.19
  266.6 0.8 copy-start.17
  267.1 1.0 copy-start.7
  320.7 1.2 copy-start.3
  323.5 1.0 copy-start.4
  323.5 1.2 copy-start.5
  323.5 1.3 copy-start.6
  323.5 1.4 copy-start.14
  325.6 0.7 copy-start.15
  327.2 1.6 copy-start.2
  402.7 1.2 copy-start.3
  405.5 1.0 copy-start.4
  405.5 1.2 copy-start.5
  405.5 1.3 copy-start.6
  405.5 1.4 copy-start.14
  407.5 0.7 copy-start.15
  409.2 1.6 copy-start.2
  485.9 1.2 copy-start.3
  488.8 1.0 copy-start.4
  488.8 1.2 copy-start.5
  488.8 1.3 copy-start.6
  488.8 1.4 copy-start.14
  490.8 0.7 copy-start.15
  492.4 1.6 copy-start.2
  571.1 1.2 copy-start.3
  574.0 1.0 copy-start.4
  574.0 1.2 copy-start.5
  574.0 1.3 copy-start.6
  574.0 1.4 copy-start.14
  577.6 1.6 copy-start.2
  656.3 1.2 copy-start.3
  659.2 1.0 copy-start.4
  659.2 1.2 copy-start.5
  659.2 1.3 copy-start.6
  659.2 1.4 copy-start.14
  661.2 0.7 copy-start.15
  662.8 1.6 copy-start.2
  741.5 1.2 copy-start.3
  744.4 1.0 copy-start.4
  744.4 1.2 copy-start.5
  744.4 1.3 copy-start.6
  744.4 1.4 copy-start.14
  746.4 0.7 copy-start.15
  748.0 1.6 copy-start.2
  790.4 1.8 copy-start.10
  790.4 1.8 copy-start.11
  792.2 13.0 %collective-permute-start.4 = (bf16[1,512,128]{2,1,0:T(8,128)(2,1)S(1)}, bf16[1,512,128]{2,1,0:T(8,128)(2,1)S(1)}, u32[]{:S(2)}, u32[]{:S(2)}) collective-permute-start(bf16[1,512,128]{2,1,0:T(8,128)(2,1)S(1)} %get-tuple-element.351), channel_id=1, source_target_pairs={{0,8},{8,16},{16,24},{24,32},{32,40},{40,48},{48,56},{56,64},{64,7... | collective-permute-start | bytes 393224 | tf_op jit(solution)/shard_map/ppermute | solution.py:21
  794.1 9.4 collective-permute-start.7
  796.0 9.1 collective-permute-start.6
  800.9 4.3 collective-permute-start.5
  817.6 150.1 %copy-start.12 = (f32[2048,128]{1,0:T(8,128)}, f32[2048,128]{1,0:T(8,128)S(1)}, u32[]{:S(2)}) copy-start(f32[2048,128]{1,0:T(8,128)S(1)} %scatter_custom_fusion.3) | copy-start | bytes 3145732
  (1 other events, 0.7 us)
Sparse Core Ops, SparseCore 0:
  802.3 156.2 all-reduce.3
where the time goes:
time: 981 us; the launch traced here: 975 us
  local copies, waits for them, and re-layouts  377 us (38%)
  other arithmetic  352 us (36%)
  waiting for transfers between devices  143 us (15%)
  matrix products  66 us (7%)
  starting transfers between devices  21.3 us (2%)
  between operations  14.6 us (1%)
    psum x1, waiting for transfers between devices, per_device(): lax.psum((edge_wgrads[0], edge_wgrads[1], edge_wgrads[2], node_sums[0], n...  141 us
    scatter-add x6, other arithmetic, backward_core(): widened_gradient.at[receiver_block].add(input_grad[:, 2 * features:])  103 us
    gather x12, local copies, waits for them, and re-layouts, inputs_of(): node_hidden_state[receiver_block]  96.1 us
    scatter-add x6, other arithmetic, backward_core(): widened_gradient.at[sender_block].add(input_grad[:, features:2 * features])  88.7 us
    scatter-add x6, other arithmetic, forward_step(): jax.ops.segment_sum(message, receiver_block, num_segments=node_rows, indi...  87.6 us
    gather x12, local copies, waits for them, and re-layouts, inputs_of(): extended[sender_block]  85 us
    gather x12, local copies, waits for them, and re-layouts, backward_core(): aggregate_grad[receiver_block]  61 us
    while x90, local copies, waits for them, and re-layouts  38.4 us
  transfers between devices with their start and end apart: 9, of which 2 were waited for; matrix products, arithmetic and copies ran while one was open for 2% of the time, Pallas kernels for 0%

commit v1 on v0

v1 whole, which is shorter than its diff:
```python
import functools
import math

import jax
import jax.numpy as jnp
from jax import lax
from jax.experimental import pallas as pl
from jax.experimental.pallas import tpu as pltpu
from jax.sharding import PartitionSpec as P

F32 = jnp.float32
BF16 = jnp.bfloat16
MESH = pl.DeviceIdType.MESH
EPS = 1e-05

D = 128
NODES = 2048
HALO = 512
EDGES = 12288
BLOCK = 1024
CHUNK = 256
BLOCKS = EDGES // BLOCK
CHUNKS = BLOCK // CHUNK
WINDOW = 256
LANES = 128
ROWS = BLOCK // LANES
PADDED = NODES + WINDOW
W_ROWS = 1280
VMEM_LIMIT = 62 * 1024 * 1024


def mm(a, b):
    return jnp.dot(a, b, preferred_element_type=F32)


def mm_t(a, b):
    return lax.dot_general(a, b, (((1,), (1,)), ((), ())), preferred_element_type=F32)


def t_mm(a, b):
    return lax.dot_general(a, b, (((0,), (0,)), ((), ())), preferred_element_type=F32)


def silu_pair(v):
    s = 0.5 * jnp.tanh(0.5 * v) + 0.5
    a = v * s
    return a.astype(BF16), (s + a * (1.0 - s)).astype(BF16)


def normalise(top):
    centred = top - jnp.mean(top, axis=-1, keepdims=True)
    inverse = lax.rsqrt(jnp.mean(centred * centred, axis=-1, keepdims=True) + EPS)
    return centred * inverse, inverse


def norm_grad(g, normed, inverse):
    return inverse * (
        g
        - jnp.mean(g, axis=-1, keepdims=True)
        - normed * jnp.mean(g * normed, axis=-1, keepdims=True)
    )


def columns_of(row):
    return jnp.transpose(jnp.broadcast_to(row, (LANES, LANES)))


def hot(mask):
    return jnp.where(mask, jnp.ones((), BF16), jnp.zeros((), BF16))


def partition_kernel(
    count_ref, recv_sm, node_ref, halo_ref, ncot_ref, edge_hbm, cot_hbm, send_ref, recv_ref,
    ewi_ref, ewm_ref, ewo_ref, nwi_ref, nwm_ref, nwo_ref,
    egrad_hbm, own_ref, border_ref, wg_ref,
    edge_v, cot_v, egrad_v, s2, rtab, agg, agtab, f2, frecv, a1, d1, a2, d2, nrm, inv, hotr, side,
    tgs, sgs, fgs, fg2, iota_r, iota_c, wge, wgm, wgo, wni, wnm, wno, sem_e, sem_c, sem_g,
):
    count = count_ref[0]

    def block_copy(hbm, v, sem, b):
        at = pl.ds(b * BLOCK, BLOCK)
        return pltpu.make_async_copy(hbm.at[at, :], v.at[at, :], sem.at[b])

    def out_copy(b):
        at = pl.ds(b * BLOCK, BLOCK)
        return pltpu.make_async_copy(egrad_v.at[at, :], egrad_hbm.at[at, :], sem_g.at[b])

    @pl.loop(0, BLOCKS)
    def _(b):
        block_copy(edge_hbm, edge_v, sem_e, b).start()

    @pl.loop(0, BLOCKS)
    def _(b):
        block_copy(cot_hbm, cot_v, sem_c, b).start()

    own_rows = pl.ds(0, NODES)
    w_e, w_s, w_r = ewi_ref[0:D], ewi_ref[D : 2 * D], ewi_ref[2 * D : 3 * D]

    @pl.loop(0, NODES // CHUNK)
    def _(i):
        at = pl.ds(i * CHUNK, CHUNK)
        s2[at, 0:D] = mm(node_ref[at, :], w_s).astype(BF16)
        s2[at, D : 2 * D] = mm(halo_ref[at, :], w_s).astype(BF16)
        rtab[at, :] = mm(node_ref[at, :], w_r).astype(BF16)
        iota_c[at, :] = (
            lax.broadcasted_iota(jnp.int32, (CHUNK, LANES), 0) + i * CHUNK
        ).astype(jnp.int16)

    iota_r[...] = lax.broadcasted_iota(jnp.int32, (16, NODES), 1).astype(jnp.int16)
    rtab[pl.ds(NODES, WINDOW), :] = jnp.zeros((WINDOW, D), BF16)
    agtab[pl.ds(NODES, WINDOW), :] = jnp.zeros((WINDOW, D), BF16)
    agg[...] = jnp.zeros_like(agg)
    frecv[...] = jnp.zeros_like(frecv)
    f2[...] = jnp.zeros_like(f2)
    for ref in (wge, wgm, wgo, wni, wnm, wno):
        ref[...] = jnp.zeros_like(ref)

    def window_of(b):
        start = pl.multiple_of((recv_sm[b * ROWS, 0] // 16) * 16, 16)
        windows = (recv_sm[b * ROWS + ROWS - 1, LANES - 1] - start) // WINDOW + 1
        return start, windows

    def tile_hot(col16, width):
        tiles = []
        for r in range(LANES // 16):
            part = col16[r * 16 : r * 16 + 16]
            tiles.append(
                jnp.concatenate(
                    [
                        hot(part == iota_r[:, t * LANES : (t + 1) * LANES])
                        for t in range(width // LANES)
                    ],
                    axis=1,
                )
            )
        return jnp.concatenate(tiles, axis=0)

    def row_hot(row, height):
        row16 = jnp.broadcast_to(row, (16, LANES)).astype(jnp.int16)
        return jnp.concatenate(
            [hot(row16 == iota_c[k * 16 : k * 16 + 16, :]) for k in range(height // 16)], axis=0
        )

    def receiver_hot(b, start, extra):
        parts = []
        for r in range(ROWS):
            row = recv_ref[pl.ds(b * ROWS + r, 1), :] - start
            place = b * BLOCK + r * LANES + lax.broadcasted_iota(jnp.int32, (1, LANES), 1)
            row = jnp.where((place < count) & (row >= 0) & (row < WINDOW), row, -1)
            parts.append(row_hot(row, WINDOW))
        return jnp.concatenate(parts, axis=1)

    def column_hot_windows(col, start, k):
        local = col - (start + k * WINDOW)
        local = jnp.where((local >= 0) & (local < WINDOW), local, -1).astype(jnp.int16)
        return tile_hot(local, WINDOW)

    def forward_block(b, single):
        start, windows = window_of(b)
        for c in range(CHUNKS):
            at = pl.ds(b * BLOCK + c * CHUNK, CHUNK)
            send_hots, recv_cols, sides = [], [], []
            for r in range(CHUNK // LANES):
                line = pl.ds(b * ROWS + c * (CHUNK // LANES) + r, 1)
                packed = columns_of(send_ref[line, :] + (recv_ref[line, :] << 12))
                sender = packed & 4095
                recv_cols.append(packed >> 12)
                sides.append(sender >= NODES)
                send_hots.append(tile_hot((sender & (NODES - 1)).astype(jnp.int16), NODES))
            picked = mm(jnp.concatenate(send_hots, axis=0), s2[...])
            far = jnp.concatenate(sides, axis=0)
            pre = jnp.where(far, picked[:, D:], picked[:, :D]) + mm(edge_v[at, :], w_e)
            side[at, :] = jnp.where(far, 1.0, 0.0).astype(BF16)
            if single:
                near = jnp.concatenate([column_hot_windows(x, start, 0) for x in recv_cols], axis=0)
                hotr[at, :] = near
                pre = pre + mm(near, rtab[pl.ds(start, WINDOW), :])
            else:

                def add(k, total):
                    near = jnp.concatenate(
                        [column_hot_windows(x, start, k) for x in recv_cols], axis=0
                    )
                    place = pl.multiple_of(start + k * WINDOW, 16)
                    return total + mm(near, rtab[pl.ds(place, WINDOW), :])

                pre = lax.fori_loop(0, windows, add, pre)
            act1, slope1 = silu_pair(pre)
            a1[at, :] = act1
            d1[at, :] = slope1
            act2, slope2 = silu_pair(mm(act1, ewm_ref[...]))
            a2[at, :] = act2
            d2[at, :] = slope2
            normed, inverse = normalise(mm(act2, ewo_ref[...]))
            nrm[at, :] = normed.astype(BF16)
            inv[at, :] = jnp.broadcast_to(inverse, (CHUNK, D))
        rows = pl.ds(b * BLOCK, BLOCK)

        def send_on(k, carry):
            place = pl.multiple_of(start + k * WINDOW, 16)
            into = pl.ds(place, WINDOW)
            agg[into, :] += mm(receiver_hot(b, place, None), nrm[rows, :])
            return carry

        if single:
            send_on(0, 0)
        else:
            lax.fori_loop(0, windows, send_on, 0)

    @pl.loop(0, BLOCKS)
    def _(b):
        block_copy(edge_hbm, edge_v, sem_e, b).wait()
        windows = window_of(b)[1]
        live = b * BLOCK < count

        @pl.when(live & (windows == 1))
        def _():
            forward_block(b, True)

        @pl.when(live & (windows > 1))
        def _():
            forward_block(b, False)

    @pl.loop(0, NODES // CHUNK)
    def _(i):
        at = pl.ds(i * CHUNK, CHUNK)
        own = node_ref[at, :]
        total = agg[at, :].astype(BF16)
        inputs = jnp.concatenate([own, total], axis=1)
        act1, slope1 = silu_pair(mm(inputs, nwi_ref[...]))
        act2, slope2 = silu_pair(mm(act1, nwm_ref[...]))
        normed, inverse = normalise(mm(act2, nwo_ref[...]))
        g = ncot_ref[at, :].astype(F32)
        top = norm_grad(g, normed, inverse).astype(BF16)
        wno[...] += t_mm(act2, top)
        second = (mm_t(top, nwo_ref[...]) * slope2.astype(F32)).astype(BF16)
        wnm[...] += t_mm(act1, second)
        first = (mm_t(second, nwm_ref[...]) * slope1.astype(F32)).astype(BF16)
        wni[...] += t_mm(inputs, first)
        back = mm_t(first, nwi_ref[...])
        own_ref[at, :] = g + back[:, :D]
        agtab[at, :] = back[:, D:].astype(BF16)

    def backward_block(b, single):
        start, windows = window_of(b)
        for c in range(CHUNKS):
            at = pl.ds(b * BLOCK + c * CHUNK, CHUNK)
            here = pl.ds(c * CHUNK, CHUNK)
            cot = cot_v[at, :].astype(F32)
            if single:
                g = cot + mm(hotr[at, :], agtab[pl.ds(start, WINDOW), :])
            else:
                cols = []
                for r in range(CHUNK // LANES):
                    line = pl.ds(b * ROWS + c * (CHUNK // LANES) + r, 1)
                    cols.append(columns_of(recv_ref[line, :]))

                def add(k, total):
                    near = jnp.concatenate([column_hot_windows(x, start, k) for x in cols], axis=0)
                    place = pl.multiple_of(start + k * WINDOW, 16)
                    return total + mm(near, agtab[pl.ds(place, WINDOW), :])

                g = lax.fori_loop(0, windows, add, cot)
            place = b * BLOCK + c * CHUNK + lax.broadcasted_iota(jnp.int32, (CHUNK, D), 0)
            live = place < count
            top = norm_grad(g, nrm[at, :].astype(F32), inv[at, :])
            top = jnp.where(live, top, 0.0).astype(BF16)
            tgs[here, :] = top
            second = (mm_t(top, ewo_ref[...]) * d2[at, :].astype(F32)).astype(BF16)
            sgs[here, :] = second
            first = (mm_t(second, ewm_ref[...]) * d1[at, :].astype(F32)).astype(BF16)
            fgs[here, :] = first
            far = first * side[at, :]
            fg2[here, D : 2 * D] = far
            fg2[here, 0:D] = first - far
            grad = cot + mm_t(first, w_e)
            egrad_v[at, :] = jnp.where(live, grad, 0.0).astype(BF16)
        out_copy(b).start()
        rows = pl.ds(b * BLOCK, BLOCK)
        wgo[...] += t_mm(a2[rows, :], tgs[...])
        wgm[...] += t_mm(a1[rows, :], sgs[...])
        wge[...] += t_mm(edge_v[rows, :], fgs[...])

        def send_on(k, carry):
            place = pl.multiple_of(start + k * WINDOW, 16)
            into = pl.ds(place, WINDOW)
            frecv[into, :] += mm(receiver_hot(b, place, None), fgs[...])
            return carry

        if single:
            send_on(0, 0)
        else:
            lax.fori_loop(0, windows, send_on, 0)
        f2[...] += mm(
            jnp.concatenate(
                [
                    row_hot(send_ref[pl.ds(b * ROWS + r, 1), :] & (NODES - 1), NODES)
                    for r in range(ROWS)
                ],
                axis=1,
            ),
            fg2[...],
        )

    @pl.loop(0, BLOCKS)
    def _(b):
        block_copy(cot_hbm, cot_v, sem_c, b).wait()
        windows = window_of(b)[1]
        live = b * BLOCK < count

        @pl.when(live & (windows == 1))
        def _():
            backward_block(b, True)

        @pl.when(live & (windows > 1))
        def _():
            backward_block(b, False)

        @pl.when(jnp.logical_not(live))
        def _():
            egrad_v[pl.ds(b * BLOCK, BLOCK), :] = jnp.zeros((BLOCK, D), BF16)
            out_copy(b).start()

    wg_ref[D : 2 * D, :] = jnp.zeros((D, D), BF16)
    wsend = jnp.zeros((D, D), F32)
    wrecv = jnp.zeros((D, D), F32)
    for i in range(NODES // BLOCK):
        at = pl.ds(i * BLOCK, BLOCK)
        near = f2[at, 0:D].astype(BF16)
        far = f2[at, D : 2 * D].astype(BF16)
        recv = frecv[at, :].astype(BF16)
        own_ref[at, :] += mm_t(near, w_s) + mm_t(recv, w_r)
        border_ref[at, :] = mm_t(far, w_s).astype(BF16)
        wsend = wsend + t_mm(node_ref[at, :], near) + t_mm(halo_ref[at, :], far)
        wrecv = wrecv + t_mm(node_ref[at, :], recv)
    wg_ref[0:D, :] = wge[...].astype(BF16)
    wg_ref[D : 2 * D, :] = wsend.astype(BF16)
    wg_ref[2 * D : 3 * D, :] = wrecv.astype(BF16)
    wg_ref[3 * D : 4 * D, :] = wgm[...].astype(BF16)
    wg_ref[4 * D : 5 * D, :] = wgo[...].astype(BF16)
    wg_ref[5 * D : 7 * D, :] = wni[...].astype(BF16)
    wg_ref[7 * D : 8 * D, :] = wnm[...].astype(BF16)
    wg_ref[8 * D : 9 * D, :] = wno[...].astype(BF16)
    wg_ref[9 * D : 10 * D, :] = jnp.zeros((D, D), BF16)

    @pl.loop(0, BLOCKS)
    def _(b):
        out_copy(b).wait()


def partition_call(count, node, halo, ncot, edge, cot, send, recv, weights):
    vm = pl.BlockSpec(memory_space=pltpu.VMEM)
    sm = pl.BlockSpec(memory_space=pltpu.SMEM)
    hb = pl.BlockSpec(memory_space=pl.ANY)
    v = pltpu.VMEM
    return pl.pallas_call(
        partition_kernel,
        out_shape=(
            jax.ShapeDtypeStruct((EDGES, D), BF16),
            jax.ShapeDtypeStruct((NODES, D), F32),
            jax.ShapeDtypeStruct((NODES, D), BF16),
            jax.ShapeDtypeStruct((W_ROWS, D), BF16),
        ),
        in_specs=[sm, sm, vm, vm, vm, hb, hb, vm, vm] + [vm] * 6,
        out_specs=(hb, vm, vm, vm),
        scratch_shapes=[
            v((EDGES, D), BF16), v((EDGES, D), BF16), v((EDGES, D), BF16),
            v((NODES, 2 * D), BF16), v((PADDED, D), BF16), v((PADDED, D), F32), v((PADDED, D), BF16),
            v((NODES, 2 * D), F32), v((PADDED, D), F32),
            v((EDGES, D), BF16), v((EDGES, D), BF16), v((EDGES, D), BF16), v((EDGES, D), BF16),
            v((EDGES, D), BF16), v((EDGES, D), F32), v((EDGES, WINDOW), BF16), v((EDGES, D), BF16),
            v((BLOCK, D), BF16), v((BLOCK, D), BF16), v((BLOCK, D), BF16), v((BLOCK, 2 * D), BF16),
            v((16, NODES), jnp.int16), v((NODES, LANES), jnp.int16),
            v((D, D), F32), v((D, D), F32), v((D, D), F32),
            v((2 * D, D), F32), v((D, D), F32), v((D, D), F32),
            pltpu.SemaphoreType.DMA((BLOCKS,)), pltpu.SemaphoreType.DMA((BLOCKS,)),
            pltpu.SemaphoreType.DMA((BLOCKS,)),
        ],
        compiler_params=pltpu.CompilerParams(vmem_limit_bytes=VMEM_LIMIT),
        name="partition",
    )(count, recv, node, halo, ncot, edge, cot, send, recv, *weights)


def cell(w, v):
    return {"wide": w, "narrow": v}


def swap_halos(w, v, wide, narrow, blocks, landing, send_sem, recv_sem):
    sides = (
        (w > 0, cell(w - 1, v)),
        (w < wide - 1, cell(w + 1, v)),
        (v > 0, cell(w, v - 1)),
        (v < narrow - 1, cell(w, v + 1)),
    )

    def copy(j):
        return pltpu.make_async_remote_copy(
            src_ref=blocks(j),
            dst_ref=landing.at[pl.ds((j ^ 1) * HALO, HALO), :],
            send_sem=send_sem.at[j],
            recv_sem=recv_sem.at[j ^ 1],
            device_id=sides[j][1],
            device_id_type=MESH,
        )

    def arrival(j):
        return pltpu.make_async_remote_copy(
            src_ref=blocks(j),
            dst_ref=landing.at[pl.ds(j * HALO, HALO), :],
            send_sem=send_sem.at[j],
            recv_sem=recv_sem.at[j],
            device_id=sides[j][1],
            device_id_type=MESH,
        )

    return sides, copy, arrival


def halo_kernel(wide, narrow, node_ref, out_rows_ref, halo_ref, outgoing, landing, send_sem, recv_sem):
    w, v = lax.axis_index("wide"), lax.axis_index("narrow")
    sides, copy, arrival = swap_halos(
        w, v, wide, narrow, lambda j: outgoing.at[pl.ds(j * HALO, HALO), :], landing, send_sem, recv_sem
    )
    barrier = pltpu.get_barrier_semaphore()
    for j in range(4):

        @pl.when(sides[j][0])
        def _():
            pl.semaphore_signal(barrier, inc=1, device_id=sides[j][1], device_id_type=MESH)

    iota = lax.broadcasted_iota(jnp.int32, (LANES, NODES), 1).astype(jnp.int16)

    def gather(j):
        hots = []
        for c in range(HALO // LANES):
            col = columns_of(out_rows_ref[j : j + 1, c * LANES : (c + 1) * LANES]).astype(jnp.int16)
            hots.append(
                jnp.concatenate(
                    [hot(col == iota[:, t * LANES : (t + 1) * LANES]) for t in range(NODES // LANES)],
                    axis=1,
                )
            )
        outgoing[pl.ds(j * HALO, HALO), :] = mm(jnp.concatenate(hots, axis=0), node_ref[...]).astype(BF16)

    for j in range(4):
        gather(j)
        if j == 0:
            peers = sum(s[0].astype(jnp.int32) for s in sides)
            pl.semaphore_wait(barrier, peers)

        @pl.when(sides[j][0])
        def _():
            copy(j).start()

    for j in range(4):
        rows = pl.ds(j * HALO, HALO)

        @pl.when(sides[j][0])
        def _():
            copy(j).wait_send()
            arrival(j).wait_recv()
            halo_ref[rows, :] = landing[rows, :]

        @pl.when(jnp.logical_not(sides[j][0]))
        def _():
            halo_ref[rows, :] = jnp.zeros((HALO, D), BF16)


def halo_call(wide, narrow, node, out_rows):
    vm = pl.BlockSpec(memory_space=pltpu.VMEM)
    return pl.pallas_call(
        functools.partial(halo_kernel, wide, narrow),
        out_shape=jax.ShapeDtypeStruct((4 * HALO, D), BF16),
        in_specs=[vm, vm],
        out_specs=vm,
        scratch_shapes=[
            pltpu.VMEM((4 * HALO, D), BF16),
            pltpu.VMEM((4 * HALO, D), BF16),
            pltpu.SemaphoreType.DMA((4,)),
            pltpu.SemaphoreType.DMA((4,)),
        ],
        compiler_params=pltpu.CompilerParams(
            collective_id=0, has_side_effects=True, vmem_limit_bytes=VMEM_LIMIT
        ),
        name="halo",
    )(node, out_rows)


def reduce_kernel(
    wide, narrow, border_ref, wg_ref, back_ref, sum_ref,
    landing, first, second, part, third, send_h, recv_h, send_1, recv_1, send_2, recv_2, send_3, recv_3,
):
    w, v = lax.axis_index("wide"), lax.axis_index("narrow")
    piece = W_ROWS // wide
    sides, copy, arrival = swap_halos(
        w, v, wide, narrow, lambda j: border_ref.at[pl.ds(j * HALO, HALO), :], landing, send_h, recv_h
    )
    barrier = pltpu.get_barrier_semaphore()
    for p in range(1, wide):
        pl.semaphore_signal(barrier, inc=1, device_id=cell(lax.rem(w + p, wide), v), device_id_type=MESH)
    for p in range(1, narrow):
        pl.semaphore_signal(barrier, inc=1, device_id=cell(w, lax.rem(v + p, narrow)), device_id_type=MESH)
    pl.semaphore_wait(barrier, wide + narrow - 2)

    def rows_of(i):
        return pl.ds(pl.multiple_of(i * piece, 16), piece)

    def send(src, dst, send_sem, recv_sem, device):
        return pltpu.make_async_remote_copy(
            src_ref=src, dst_ref=dst, send_sem=send_sem, recv_sem=recv_sem, device_id=device,
            device_id_type=MESH,
        )

    scatter, share, spread = [], [], []
    for p in range(1, wide):
        to = lax.rem(w + p, wide)
        scatter.append(
            send(wg_ref.at[rows_of(to), :], first.at[p], send_1.at[p], recv_1.at[p], cell(to, v))
        )
        scatter[-1].start()
    for j in range(4):

        @pl.when(sides[j][0])
        def _():
            copy(j).start()

    total = wg_ref[rows_of(w), :].astype(F32)
    for p in range(1, wide):
        scatter[p - 1].wait_recv()
        total = total + first[p].astype(F32)
    part[...] = total.astype(BF16)
    for p in range(1, narrow):
        to = lax.rem(v + p, narrow)
        share.append(send(part, second.at[v], send_2.at[p], recv_2.at[p], cell(w, to)))
        share[-1].start()
    second[v] = part[...]
    for p in range(1, narrow):
        share[p - 1].wait_recv()
    total = second[0].astype(F32)
    for i in range(1, narrow):
        total = total + second[i].astype(F32)
    third[rows_of(w), :] = total.astype(BF16)
    for p in range(1, wide):
        to = lax.rem(w + p, wide)
        spread.append(
            send(
                third.at[rows_of(w), :], third.at[rows_of(w), :], send_3.at[p], recv_3.at[p], cell(to, v)
            )
        )
        spread[-1].start()
    for j in range(4):
        rows = pl.ds(j * HALO, HALO)

        @pl.when(sides[j][0])
        def _():
            copy(j).wait_send()
            arrival(j).wait_recv()
            back_ref[rows, :] = landing[rows, :]

        @pl.when(jnp.logical_not(sides[j][0]))
        def _():
            back_ref[rows, :] = jnp.zeros((HALO, D), BF16)

    for p in range(1, wide):
        spread[p - 1].wait_recv()
    sum_ref[...] = third[...]
    for c in scatter + share + spread:
        c.wait_send()


def reduce_call(wide, narrow, border, wg):
    vm = pl.BlockSpec(memory_space=pltpu.VMEM)
    piece = W_ROWS // wide
    sem = pltpu.SemaphoreType.DMA
    return pl.pallas_call(
        functools.partial(reduce_kernel, wide, narrow),
        out_shape=(
            jax.ShapeDtypeStruct((4 * HALO, D), BF16),
            jax.ShapeDtypeStruct((W_ROWS, D), BF16),
        ),
        in_specs=[vm, vm],
        out_specs=(vm, vm),
        scratch_shapes=[
            pltpu.VMEM((4 * HALO, D), BF16),
            pltpu.VMEM((wide, piece, D), BF16),
            pltpu.VMEM((narrow, piece, D), BF16),
            pltpu.VMEM((piece, D), BF16),
            pltpu.VMEM((W_ROWS, D), BF16),
            sem((4,)), sem((4,)), sem((wide,)), sem((wide,)), sem((narrow,)), sem((narrow,)),
            sem((wide,)), sem((wide,)),
        ],
        compiler_params=pltpu.CompilerParams(
            collective_id=1, has_side_effects=True, vmem_limit_bytes=VMEM_LIMIT
        ),
        name="reduce",
    )(border, wg)


def finish_kernel(scales, out_rows_ref, own_ref, back_ref, sum_ref, node_ref, *outs):
    for i in range(NODES // CHUNK):
        at = pl.ds(i * CHUNK, CHUNK)
        iota = (lax.broadcasted_iota(jnp.int32, (CHUNK, LANES), 0) + i * CHUNK).astype(jnp.int16)
        hots = []
        for j in range(4):
            for c in range(HALO // LANES):
                row = out_rows_ref[j : j + 1, c * LANES : (c + 1) * LANES]
                row16 = jnp.broadcast_to(row, (CHUNK, LANES)).astype(jnp.int16)
                hots.append(hot(row16 == iota))
        node_ref[at, :] = own_ref[at, :] + mm(jnp.concatenate(hots, axis=1), back_ref[...])
    at = 0
    for out, scale in zip(outs, scales):
        rows = out.shape[0]
        out[...] = sum_ref[at : at + rows, :].astype(F32) * scale
        at += rows


def finish_call(scales, out_rows, own, back, summed, shapes):
    vm = pl.BlockSpec(memory_space=pltpu.VMEM)
    return pl.pallas_call(
        functools.partial(finish_kernel, scales),
        out_shape=(jax.ShapeDtypeStruct((NODES, D), F32),)
        + tuple(jax.ShapeDtypeStruct(s, F32) for s in shapes),
        in_specs=[vm] * 4,
        out_specs=(vm,) * 7,
        compiler_params=pltpu.CompilerParams(vmem_limit_bytes=VMEM_LIMIT),
        name="finish",
    )(out_rows, own, back, summed)


def per_device(
    wide,
    narrow,
    node_hidden_state,
    edge_hidden_state,
    node_output_gradient,
    edge_output_gradient,
    senders,
    receivers,
    edge_slot_count,
    outbound_rows,
    *weights,
):
    out_rows = outbound_rows.reshape(4, HALO)
    halo = halo_call(wide, narrow, node_hidden_state, out_rows)
    edge_grad, own, border, wg = partition_call(
        edge_slot_count,
        node_hidden_state,
        halo,
        node_output_gradient,
        edge_hidden_state,
        edge_output_gradient,
        senders.reshape(EDGES // LANES, LANES),
        receivers.reshape(EDGES // LANES, LANES),
        weights,
    )
    back, summed = reduce_call(wide, narrow, border, wg)
    edge_scale = 1.0 / math.sqrt(EDGES * wide * narrow)
    node_scale = 1.0 / math.sqrt(NODES * wide * narrow)
    node_grad, *sums = finish_call(
        (edge_scale,) * 3 + (node_scale,) * 3, out_rows, own, back, summed, [x.shape for x in weights]
    )
    return (node_grad, edge_grad, *sums)


def solution(mesh):
    both = ("wide", "narrow")
    rows, flat = P(both, None), P(both)
    return jax.shard_map(
        functools.partial(per_device, mesh.shape["wide"], mesh.shape["narrow"]),
        mesh=mesh,
        in_specs=(rows, rows, rows, rows, flat, flat, flat, P(both, None, None)) + (P(),) * 6,
        out_specs=(rows, rows) + (P(),) * 6,
        check_vma=False,
    )
```

time: 981 us -> 152 us (0.15)
  local copies, waits for them, and re-layouts: 377 us -> 0 us
  other arithmetic: 352 us -> 0 us
  Pallas kernels: 0 us -> 148 us
  waiting for transfers between devices: 143 us -> 0 us
  matrix products: 66 us -> 0 us
  starting transfers between devices: 21.3 us -> 0 us
  between operations: 14.6 us -> 1.3 us
    scatter-add x19 -> x0, other arithmetic: 292 us -> none  [the longest x6 103 us: backward_core(): widened_gradient.at[receiver_block].add(input_grad[:, 2 * features:])]
    gather x37 -> x0, local copies, waits for them, and re-layouts: 249 us -> none  [the longest x12 96.1 us: inputs_of(): node_hidden_state[receiver_block]]
    pallas_call x0 -> x4, Pallas kernels: none -> 148 us  [the longest x1 64.5 us: reduce_call(): pl.pallas_call(functools.partial(reduce_kernel, wide, narrow), out_shape=...]
    psum x1 -> x0, waiting for transfers between devices: 141 us -> none  [per_device(): lax.psum((edge_wgrads[0], edge_wgrads[1], edge_wgrads[2], node_sums[0], n...]
    dot_general x75 -> x0, matrix products: 66 us -> none  [the longest x13 20.6 us: mlp_forward(): jnp.dot(first_act, weight_mid, preferred_element_type=jnp.float32)]
    while x90 -> x0, local copies, waits for them, and re-layouts: 38.4 us -> none
    dynamic_slice x24 -> x0, local copies, waits for them, and re-layouts: 25.7 us -> none  [per_device(): lax.scan(forward_step, jnp.zeros((node_rows, features), jnp.float32), (la...]
    squeeze x12 -> x0, local copies, waits for them, and re-layouts: 22.4 us -> none  [per_device(): lax.scan(forward_step, jnp.zeros((node_rows, features), jnp.float32), (la...]
  transfers between devices with their start and end apart: 9 -> 0, of which waited for: 2 -> 0; matrix products, arithmetic and copies ran while one was open for 2% -> 0% of each run, Pallas kernels for 0% -> 0%
where the time goes in v1:
time: 152 us; the launch traced here: 150 us
  Pallas kernels  148 us (97%)
    pallas_call x1, Pallas kernels, reduce_call(): pl.pallas_call(functools.partial(reduce_kernel, wide, narrow), out_shape=...  64.5 us
    pallas_call x1, Pallas kernels, partition_call(): pl.pallas_call(partition_kernel, out_shape=(jax.ShapeDtypeStruct((EDGES,...  64.1 us
    pallas_call x1, Pallas kernels, halo_call(): pl.pallas_call(functools.partial(halo_kernel, wide, narrow), out_shape=ja...  15 us
    pallas_call x1, Pallas kernels, finish_call(): pl.pallas_call(functools.partial(finish_kernel, scales), out_shape=(jax.S...  4.93 us

profile of v1, /device:TPU:32, one launch (start us, length us, event | category | flops | bytes accessed | tf_op | source)
XLA Modules:
  0.0 149.7 jit_solution(3032307113898324766)
XLA Ops:
  1.3 15.0 %halo.1.halo_ref = bf16[2048,128]{1,0:T(8,128)(2,1)} custom-call(bf16[2048,128]{1,0:T(8,128)(2,1)} %node_ref.3, s32[4,512]{1,0:T(4,128)} %bitcast.6), custom_call_target="tpu_custom_call" | custom-call | tf_op jit(solution)/shard_map/halo/pallas_call | solution.py:472
  16.3 64.1 %partition.1 = (bf16[12288,128]{1,0:T(8,128)(2,1)}, f32[2048,128]{1,0:T(8,128)}, bf16[2048,128]{1,0:T(8,128)(2,1)}, bf16[1280,128]{1,0:T(8,128)(2,1)}) custom-call(s32[1]{0:T(128)S(6)} %copy.22.count_ref, s32[96,128]{1,0:T(8,128)} %bitcast.3, bf16[2048,128]{1,0:T(8,128)(2,1)} %node_ref.3, bf16[2048,128]{1,0:T(8,128)(2,1)} %halo.1.halo_ref, ...), custom_call_target="tpu_custom_call" | custom-call | tf_op jit(solution)/shard_map/partition/pallas_call | solution.py:357
  80.3 64.5 %reduce.1 = (bf16[2048,128]{1,0:T(8,128)(2,1)}, bf16[1280,128]{1,0:T(8,128)(2,1)}) custom-call(bf16[2048,128]{1,0:T(8,128)(2,1)} %get-tuple-element.22.border_ref, bf16[1280,128]{1,0:T(8,128)(2,1)} %get-tuple-element.23.wg_ref), custom_call_target="tpu_custom_call" | custom-call | tf_op jit(solution)/shard_map/reduce/pallas_call | solution.py:576
  144.8 4.9 %finish.1 = (f32[2048,128]{1,0:T(8,128)}, f32[384,128]{1,0:T(8,128)}, f32[128,128]{1,0:T(8,128)}, f32[128,128]{1,0:T(8,128)}, f32[256,128]{1,0:T(8,128)}, /*index=5*/f32[128,128]{1,0:T(8,128)}, f32[128,128]{1,0:T(8,128)}) custom-call(s32[4,512]{1,0:T(4,128)} %bitcast.7, f32[2048,128]{1,0:T(8,128)} %get-tuple-element.21.own_ref, ...), custom_call_target="tpu_custom_call" | custom-call | tf_op jit(solution)/shard_map/finish/pallas_call | solution.py:620

commit v2 on v1

v2 whole, which is shorter than its diff:
```python
import functools
import math

import jax
import jax.numpy as jnp
from jax import lax
from jax.experimental import pallas as pl
from jax.experimental.pallas import tpu as pltpu
from jax.sharding import PartitionSpec as P

F32 = jnp.float32
BF16 = jnp.bfloat16
MESH = pl.DeviceIdType.MESH
EPS = 1e-05

D = 128
NODES = 2048
HALO = 512
EDGES = 12288
BLOCK = 1024
CHUNK = 1024
NODE_CHUNK = 1024
BLOCKS = EDGES // BLOCK
CHUNKS = BLOCK // CHUNK
WINDOW = 256
LANES = 128
ROWS = BLOCK // LANES
PADDED = NODES + WINDOW
W_ROWS = 1280
EARLY = 4
VMEM_LIMIT = 62 * 1024 * 1024


def mm(a, b):
    return jnp.dot(a, b, preferred_element_type=F32)


def mm_t(a, b):
    return lax.dot_general(a, b, (((1,), (1,)), ((), ())), preferred_element_type=F32)


def t_mm(a, b):
    return lax.dot_general(a, b, (((0,), (0,)), ((), ())), preferred_element_type=F32)


def silu_pair(v):
    s = 0.5 * jnp.tanh(0.5 * v) + 0.5
    a = v * s
    return a.astype(BF16), (s + a * (1.0 - s)).astype(BF16)


def normalise(top):
    centred = top - jnp.mean(top, axis=-1, keepdims=True)
    inverse = lax.rsqrt(jnp.mean(centred * centred, axis=-1, keepdims=True) + EPS)
    return centred * inverse, inverse


def norm_grad(g, normed, inverse):
    return inverse * (
        g
        - jnp.mean(g, axis=-1, keepdims=True)
        - normed * jnp.mean(g * normed, axis=-1, keepdims=True)
    )


def columns_of(row):
    return jnp.transpose(jnp.broadcast_to(row, (LANES, LANES)))


def hot(mask):
    return jnp.where(mask, jnp.ones((), BF16), jnp.zeros((), BF16))


def partition_kernel(
    count_ref, recv_sm, node_ref, ncot_ref, edge_hbm, cot_hbm, picked_hbm, recv_ref,
    ewi_ref, ewm_ref, ewo_ref, nwi_ref, nwm_ref, nwo_ref,
    egrad_hbm, first_hbm, own_ref, wg_ref,
    edge_v, cot_v, picked_v, first_v, rtab, agg, agtab, frecv, a1, d1, a2, d2, nrm, inv, hotr,
    tgs, sgs, iota_r, iota_c, wge, wgm, wgo, wni, wnm, wno, sem_e, sem_c, sem_p, sem_g, sem_f,
):
    count = count_ref[0]

    def block_copy(hbm, v, sem, b):
        at = pl.ds(b * BLOCK, BLOCK)
        return pltpu.make_async_copy(hbm.at[at, :], v.at[at, :], sem.at[b])

    def out_copy(b):
        at = pl.ds(b * BLOCK, BLOCK)
        return pltpu.make_async_copy(cot_v.at[at, :], egrad_hbm.at[at, :], sem_g.at[b])

    def first_copy(b):
        at = pl.ds(b * BLOCK, BLOCK)
        return pltpu.make_async_copy(first_v.at[at, :], first_hbm.at[at, :], sem_f.at[b])

    @pl.loop(0, BLOCKS)
    def _(b):
        block_copy(edge_hbm, edge_v, sem_e, b).start()
        block_copy(picked_hbm, picked_v, sem_p, b).start()

    @pl.loop(0, BLOCKS)
    def _(b):
        block_copy(cot_hbm, cot_v, sem_c, b).start()

    w_e, w_es, w_r = ewi_ref[0:D], ewi_ref[0 : 2 * D], ewi_ref[2 * D : 3 * D]

    for i in range(NODES // NODE_CHUNK):
        at = pl.ds(i * NODE_CHUNK, NODE_CHUNK)
        rtab[at, :] = mm(node_ref[at, :], w_r).astype(BF16)

    iota_r[...] = lax.broadcasted_iota(jnp.int32, (16, WINDOW), 1).astype(jnp.int16)
    iota_c[...] = lax.broadcasted_iota(jnp.int32, (WINDOW, LANES), 0).astype(jnp.int16)
    rtab[pl.ds(NODES, WINDOW), :] = jnp.zeros((WINDOW, D), BF16)
    agtab[pl.ds(NODES, WINDOW), :] = jnp.zeros((WINDOW, D), BF16)
    agg[...] = jnp.zeros_like(agg)
    frecv[...] = jnp.zeros_like(frecv)
    for ref in (wge, wgm, wgo, wni, wnm, wno):
        ref[...] = jnp.zeros_like(ref)

    def window_of(b):
        start = pl.multiple_of((recv_sm[b * ROWS, 0] // 16) * 16, 16)
        windows = (recv_sm[b * ROWS + ROWS - 1, LANES - 1] - start) // WINDOW + 1
        return start, windows

    def tile_hot(col16, width):
        tiles = []
        for r in range(LANES // 16):
            part = col16[r * 16 : r * 16 + 16]
            tiles.append(
                jnp.concatenate(
                    [
                        hot(part == iota_r[:, t * LANES : (t + 1) * LANES])
                        for t in range(width // LANES)
                    ],
                    axis=1,
                )
            )
        return jnp.concatenate(tiles, axis=0)

    def row_hot(row, height):
        row16 = jnp.broadcast_to(row, (16, LANES)).astype(jnp.int16)
        return jnp.concatenate(
            [hot(row16 == iota_c[k * 16 : k * 16 + 16, :]) for k in range(height // 16)], axis=0
        )

    def receiver_hot(b, start, extra):
        parts = []
        for r in range(ROWS):
            row = recv_ref[pl.ds(b * ROWS + r, 1), :] - start
            place = b * BLOCK + r * LANES + lax.broadcasted_iota(jnp.int32, (1, LANES), 1)
            row = jnp.where((place < count) & (row >= 0) & (row < WINDOW), row, -1)
            parts.append(row_hot(row, WINDOW))
        return jnp.concatenate(parts, axis=1)

    def column_hot_windows(col, start, k):
        local = col - (start + k * WINDOW)
        local = jnp.where((local >= 0) & (local < WINDOW), local, -1).astype(jnp.int16)
        return tile_hot(local, WINDOW)

    def forward_block(b, single):
        start, windows = window_of(b)
        for c in range(CHUNKS):
            at = pl.ds(b * BLOCK + c * CHUNK, CHUNK)
            recv_cols = []
            for r in range(CHUNK // LANES):
                line = pl.ds(b * ROWS + c * (CHUNK // LANES) + r, 1)
                recv_cols.append(columns_of(recv_ref[line, :]))
            pre = mm(jnp.concatenate([edge_v[at, :], picked_v[at, :]], axis=1), w_es)
            if single:
                near = jnp.concatenate([column_hot_windows(x, start, 0) for x in recv_cols], axis=0)
                hotr[at, :] = near
                pre = pre + mm(near, rtab[pl.ds(start, WINDOW), :])
            else:

                def add(k, total):
                    near = jnp.concatenate(
                        [column_hot_windows(x, start, k) for x in recv_cols], axis=0
                    )
                    place = pl.multiple_of(start + k * WINDOW, 16)
                    return total + mm(near, rtab[pl.ds(place, WINDOW), :])

                pre = lax.fori_loop(0, windows, add, pre)
            act1, slope1 = silu_pair(pre)
            a1[at, :] = act1
            d1[at, :] = slope1
            act2, slope2 = silu_pair(mm(act1, ewm_ref[...]))
            a2[at, :] = act2
            d2[at, :] = slope2
            normed, inverse = normalise(mm(act2, ewo_ref[...]))
            nrm[at, :] = normed.astype(BF16)
            inv[at, :] = jnp.broadcast_to(inverse, (CHUNK, D)).astype(BF16)
        rows = pl.ds(b * BLOCK, BLOCK)

        def send_on(k, carry):
            place = pl.multiple_of(start + k * WINDOW, 16)
            into = pl.ds(place, WINDOW)
            agg[into, :] += mm(receiver_hot(b, place, None), nrm[rows, :])
            return carry

        if single:
            send_on(0, 0)
        else:
            lax.fori_loop(0, windows, send_on, 0)

    @pl.loop(0, BLOCKS)
    def _(b):
        block_copy(edge_hbm, edge_v, sem_e, b).wait()
        block_copy(picked_hbm, picked_v, sem_p, b).wait()
        windows = window_of(b)[1]
        live = b * BLOCK < count

        @pl.when(live & (windows == 1))
        def _():
            forward_block(b, True)

        @pl.when(live & (windows > 1))
        def _():
            forward_block(b, False)

    @pl.loop(0, NODES // NODE_CHUNK)
    def _(i):
        at = pl.ds(i * NODE_CHUNK, NODE_CHUNK)
        own = node_ref[at, :]
        total = agg[at, :].astype(BF16)
        inputs = jnp.concatenate([own, total], axis=1)
        act1, slope1 = silu_pair(mm(inputs, nwi_ref[...]))
        act2, slope2 = silu_pair(mm(act1, nwm_ref[...]))
        normed, inverse = normalise(mm(act2, nwo_ref[...]))
        g = ncot_ref[at, :].astype(F32)
        top = norm_grad(g, normed, inverse).astype(BF16)
        wno[...] += t_mm(act2, top)
        second = (mm_t(top, nwo_ref[...]) * slope2.astype(F32)).astype(BF16)
        wnm[...] += t_mm(act1, second)
        first = (mm_t(second, nwm_ref[...]) * slope1.astype(F32)).astype(BF16)
        wni[...] += t_mm(inputs, first)
        back = mm_t(first, nwi_ref[...])
        own_ref[at, :] = g + back[:, :D]
        agtab[at, :] = back[:, D:].astype(BF16)

    def backward_block(b, single):
        start, windows = window_of(b)
        for c in range(CHUNKS):
            at = pl.ds(b * BLOCK + c * CHUNK, CHUNK)
            here = pl.ds(c * CHUNK, CHUNK)
            cot = cot_v[at, :].astype(F32)
            if single:
                g = cot + mm(hotr[at, :], agtab[pl.ds(start, WINDOW), :])
            else:
                cols = []
                for r in range(CHUNK // LANES):
                    line = pl.ds(b * ROWS + c * (CHUNK // LANES) + r, 1)
                    cols.append(columns_of(recv_ref[line, :]))

                def add(k, total):
                    near = jnp.concatenate([column_hot_windows(x, start, k) for x in cols], axis=0)
                    place = pl.multiple_of(start + k * WINDOW, 16)
                    return total + mm(near, agtab[pl.ds(place, WINDOW), :])

                g = lax.fori_loop(0, windows, add, cot)
            place = b * BLOCK + c * CHUNK + lax.broadcasted_iota(jnp.int32, (CHUNK, D), 0)
            live = place < count
            top = norm_grad(g, nrm[at, :].astype(F32), inv[at, :].astype(F32))
            top = jnp.where(live, top, 0.0).astype(BF16)
            tgs[here, :] = top
            second = (mm_t(top, ewo_ref[...]) * d2[at, :].astype(F32)).astype(BF16)
            sgs[here, :] = second
            first = (mm_t(second, ewm_ref[...]) * d1[at, :].astype(F32)).astype(BF16)
            first_v[at, :] = first
            grad = cot + mm_t(first, w_e)
            cot_v[at, :] = jnp.where(live, grad, 0.0).astype(BF16)
        out_copy(b).start()
        first_copy(b).start()
        rows = pl.ds(b * BLOCK, BLOCK)
        wgo[...] += t_mm(a2[rows, :], tgs[...])
        wgm[...] += t_mm(a1[rows, :], sgs[...])
        wge[0:D, :] += t_mm(edge_v[rows, :], first_v[rows, :])
        wge[D : 2 * D, :] += t_mm(picked_v[rows, :], first_v[rows, :])

        def send_on(k, carry):
            place = pl.multiple_of(start + k * WINDOW, 16)
            into = pl.ds(place, WINDOW)
            frecv[into, :] += mm(receiver_hot(b, place, None), first_v[rows, :])
            return carry

        if single:
            send_on(0, 0)
        else:
            lax.fori_loop(0, windows, send_on, 0)

    @pl.loop(0, BLOCKS)
    def _(b):
        block_copy(cot_hbm, cot_v, sem_c, b).wait()
        windows = window_of(b)[1]
        live = b * BLOCK < count

        @pl.when(live & (windows == 1))
        def _():
            backward_block(b, True)

        @pl.when(live & (windows > 1))
        def _():
            backward_block(b, False)

        @pl.when(jnp.logical_not(live))
        def _():
            cot_v[pl.ds(b * BLOCK, BLOCK), :] = jnp.zeros((BLOCK, D), BF16)
            first_v[pl.ds(b * BLOCK, BLOCK), :] = jnp.zeros((BLOCK, D), BF16)
            out_copy(b).start()
            first_copy(b).start()

    wrecv = jnp.zeros((D, D), F32)
    for i in range(NODES // NODE_CHUNK):
        at = pl.ds(i * NODE_CHUNK, NODE_CHUNK)
        recv = frecv[at, :].astype(BF16)
        own_ref[at, :] += mm_t(recv, w_r)
        wrecv = wrecv + t_mm(node_ref[at, :], recv)
    wg_ref[0 : 2 * D, :] = wge[...].astype(BF16)
    wg_ref[2 * D : 3 * D, :] = wrecv.astype(BF16)
    wg_ref[3 * D : 4 * D, :] = wgm[...].astype(BF16)
    wg_ref[4 * D : 5 * D, :] = wgo[...].astype(BF16)
    wg_ref[5 * D : 7 * D, :] = wni[...].astype(BF16)
    wg_ref[7 * D : 8 * D, :] = wnm[...].astype(BF16)
    wg_ref[8 * D : 9 * D, :] = wno[...].astype(BF16)
    wg_ref[9 * D : 10 * D, :] = jnp.zeros((D, D), BF16)

    @pl.loop(0, BLOCKS)
    def _(b):
        out_copy(b).wait()
        first_copy(b).wait()


def partition_call(count, node, ncot, edge, cot, picked, recv, weights):
    vm = pl.BlockSpec(memory_space=pltpu.VMEM)
    sm = pl.BlockSpec(memory_space=pltpu.SMEM)
    hb = pl.BlockSpec(memory_space=pl.ANY)
    v = pltpu.VMEM
    return pl.pallas_call(
        partition_kernel,
        out_shape=(
            jax.ShapeDtypeStruct((EDGES, D), BF16),
            jax.ShapeDtypeStruct((EDGES, D), BF16),
            jax.ShapeDtypeStruct((NODES, D), F32),
            jax.ShapeDtypeStruct((W_ROWS, D), BF16),
        ),
        in_specs=[sm, sm, vm, vm, hb, hb, hb, vm] + [vm] * 6,
        out_specs=(hb, hb, vm, vm),
        scratch_shapes=[
            v((EDGES, D), BF16), v((EDGES, D), BF16), v((EDGES, D), BF16), v((EDGES, D), BF16),
            v((PADDED, D), BF16), v((PADDED, D), F32), v((PADDED, D), BF16), v((PADDED, D), F32),
            v((EDGES, D), BF16), v((EDGES, D), BF16), v((EDGES, D), BF16), v((EDGES, D), BF16),
            v((EDGES, D), BF16), v((EDGES, D), BF16), v((EDGES, WINDOW), BF16),
            v((BLOCK, D), BF16), v((BLOCK, D), BF16),
            v((16, WINDOW), jnp.int16), v((WINDOW, LANES), jnp.int16),
            v((2 * D, D), F32), v((D, D), F32), v((D, D), F32),
            v((2 * D, D), F32), v((D, D), F32), v((D, D), F32),
        ] + [pltpu.SemaphoreType.DMA((BLOCKS,))] * 5,
        compiler_params=pltpu.CompilerParams(vmem_limit_bytes=VMEM_LIMIT),
        name="partition",
    )(count, recv, node, ncot, edge, cot, picked, recv, *weights)


def cell(w, v):
    return {"wide": w, "narrow": v}


def swap_halos(w, v, wide, narrow, blocks, landing, send_sem, recv_sem):
    sides = (
        (w > 0, cell(w - 1, v)),
        (w < wide - 1, cell(w + 1, v)),
        (v > 0, cell(w, v - 1)),
        (v < narrow - 1, cell(w, v + 1)),
    )

    def transfer(j, slot):
        return pltpu.make_async_remote_copy(
            src_ref=blocks.at[pl.ds(j * HALO, HALO), :],
            dst_ref=landing.at[pl.ds(slot * HALO, HALO), :],
            send_sem=send_sem.at[j],
            recv_sem=recv_sem.at[slot],
            device_id=sides[j][1],
            device_id_type=MESH,
        )

    def start(j):
        @pl.when(sides[j][0])
        def _():
            transfer(j, j ^ 1).start()

    def finish(j):
        @pl.when(sides[j][0])
        def _():
            transfer(j, j ^ 1).wait_send()
            transfer(j, j).wait_recv()

        @pl.when(jnp.logical_not(sides[j][0]))
        def _():
            landing[pl.ds(j * HALO, HALO), :] = jnp.zeros((HALO, D), BF16)

    def greet(barrier):
        for there, device in sides:

            @pl.when(there)
            def _():
                pl.semaphore_signal(barrier, inc=1, device_id=device, device_id_type=MESH)

        return sum(there.astype(jnp.int32) for there, _ in sides)

    return greet, start, finish


def column_hot(cols, iota, width):
    return jnp.concatenate(
        [hot(cols == iota[:, t * LANES : (t + 1) * LANES]) for t in range(width // LANES)], axis=1
    )


def gather_kernel(
    wide, narrow, node_ref, out_rows_ref, send_ref, picked_hbm,
    outgoing, landing, table, iota_ref, held, send_sem, recv_sem, out_sem,
):
    w, v = lax.axis_index("wide"), lax.axis_index("narrow")
    greet, start, finish = swap_halos(w, v, wide, narrow, outgoing, landing, send_sem, recv_sem)
    barrier = pltpu.get_barrier_semaphore()
    peers = greet(barrier)
    iota_ref[...] = lax.broadcasted_iota(jnp.int32, (LANES, NODES), 1).astype(jnp.int16)
    half = NODES // 2
    table[0:half, 0:D] = node_ref[0:half, :]
    table[0:half, D : 2 * D] = node_ref[half:NODES, :]

    for j in range(4):
        hots, high = [], []
        for c in range(HALO // LANES):
            col = columns_of(out_rows_ref[j : j + 1, c * LANES : (c + 1) * LANES])
            high.append(col >= half)
            hots.append(column_hot((col & (half - 1)).astype(jnp.int16), iota_ref, half))
        both = mm(jnp.concatenate(hots, axis=0), table[0:half, :])
        rows = jnp.where(jnp.concatenate(high, axis=0), both[:, D:], both[:, :D])
        outgoing[pl.ds(j * HALO, HALO), :] = rows.astype(BF16)
        if j == 0:
            pl.semaphore_wait(barrier, peers)
        start(j)

    def out_copy(b):
        at = pl.ds(b * BLOCK, BLOCK)
        return pltpu.make_async_copy(held.at[at, :], picked_hbm.at[at, :], out_sem.at[b])

    def pick(b, own, far):
        hots, high = [], []
        for r in range(ROWS):
            col = columns_of(send_ref[pl.ds(b * ROWS + r, 1), :])
            high.append((col & half) != 0)
            place = (col & (half - 1)) + jnp.where(col >= NODES, half, 0)
            if not own:
                place = place - half
            hots.append(column_hot(place.astype(jnp.int16), iota_ref, half * (own + far)))
        lower = 0 if own else half
        both = mm(jnp.concatenate(hots, axis=0), table[lower : lower + half * (own + far), :])
        return jnp.where(jnp.concatenate(high, axis=0), both[:, D:], both[:, :D]).astype(BF16)

    @pl.loop(0, EARLY)
    def _(b):
        held[pl.ds(b * BLOCK, BLOCK), :] = pick(b, True, False)

    for j in range(4):
        finish(j)
    table[half:NODES, 0:D] = landing[0:half, :]
    table[half:NODES, D : 2 * D] = landing[half:NODES, :]

    @pl.loop(0, EARLY)
    def _(b):
        held[pl.ds(b * BLOCK, BLOCK), :] += pick(b, False, True)
        out_copy(b).start()

    @pl.loop(EARLY, BLOCKS)
    def _(b):
        held[pl.ds(b * BLOCK, BLOCK), :] = pick(b, True, True)
        out_copy(b).start()

    @pl.loop(0, BLOCKS)
    def _(b):
        out_copy(b).wait()


def gather_call(wide, narrow, node, out_rows, send):
    vm = pl.BlockSpec(memory_space=pltpu.VMEM)
    sem = pltpu.SemaphoreType.DMA
    return pl.pallas_call(
        functools.partial(gather_kernel, wide, narrow),
        out_shape=jax.ShapeDtypeStruct((EDGES, D), BF16),
        in_specs=[vm, vm, vm],
        out_specs=pl.BlockSpec(memory_space=pl.ANY),
        scratch_shapes=[
            pltpu.VMEM((4 * HALO, D), BF16),
            pltpu.VMEM((4 * HALO, D), BF16),
            pltpu.VMEM((NODES, 2 * D), BF16),
            pltpu.VMEM((LANES, NODES), jnp.int16),
            pltpu.VMEM((EDGES, D), BF16),
            sem((4,)), sem((4,)), sem((BLOCKS,)),
        ],
        compiler_params=pltpu.CompilerParams(
            collective_id=0, has_side_effects=True, vmem_limit_bytes=VMEM_LIMIT
        ),
        name="gather",
    )(node, out_rows, send)


def scatter_kernel(
    wide, narrow, first_hbm, send_ref, own_ref, wg_ref, ewi_ref, out_rows_ref, node_ref, sum_ref,
    first_v, f2, iota_c, border, landing, pair, half, quarter, part, along_z, other, along_x, third,
    first_sem, send_h, recv_h, send_a, recv_a,
):
    w, v = lax.axis_index("wide"), lax.axis_index("narrow")
    y, zh, core = w // 4, (w // 2) % 2, w % 2
    x, zl = v // 2, v % 2
    z = zh * 2 + zl
    n_half, n_quarter = W_ROWS // 2, W_ROWS // 8

    def block_copy(b):
        at = pl.ds(b * BLOCK, BLOCK)
        return pltpu.make_async_copy(first_hbm.at[at, :], first_v.at[at, :], first_sem.at[b])

    @pl.loop(0, BLOCKS)
    def _(b):
        block_copy(b).start()

    greet, start, finish = swap_halos(w, v, wide, narrow, border, landing, send_h, recv_h)

    def rank(y, zh, core, x, zl):
        return cell(y * 4 + zh * 2 + core, x * 2 + zl)

    partner = rank(y, zh, 1 - core, x, zl)
    y_peers = [((y + i) % 4, rank((y + i) % 4, zh, core, x, zl)) for i in range(1, 4)]
    z_peers = [rank(y, (zh + i) % 2, core, x, (zl + j) % 2) for i, j in ((0, 1), (1, 0), (1, 1))]
    x_peers = [rank(y, zh, core, (x + i) % 4, zl) for i in range(1, 4)]
    barrier = pltpu.get_barrier_semaphore()
    peers = greet(barrier)
    others = [partner] + [d for _, d in y_peers] + z_peers + x_peers
    for device in others:
        pl.semaphore_signal(barrier, inc=1, device_id=device, device_id_type=MESH)

    iota_c[...] = lax.broadcasted_iota(jnp.int32, (NODES, LANES), 0).astype(jnp.int16)
    f2[...] = jnp.zeros_like(f2)
    pl.semaphore_wait(barrier, peers + len(others))

    def send(i, src, dst, device):
        return pltpu.make_async_remote_copy(
            src_ref=src, dst_ref=dst, send_sem=send_a.at[i], recv_sem=recv_a.at[i], device_id=device,
            device_id_type=MESH,
        )

    def half_rows(i):
        return pl.ds(pl.multiple_of(i * n_half, 16), n_half)

    def quarter_rows(i):
        return pl.ds(pl.multiple_of(i * n_quarter, 16), n_quarter)

    def mine():
        return pl.ds(pl.multiple_of(core * n_half + y * n_quarter, 16), n_quarter)

    def scatter(lo, hi):
        @pl.loop(lo, hi)
        def _(b):
            block_copy(b).wait()
            rows = pl.ds(b * BLOCK, BLOCK)
            value = first_v[rows, :]
            far, hots = [], []
            for r in range(ROWS):
                line = send_ref[pl.ds(b * ROWS + r, 1), :]
                far.append(hot(columns_of(line) >= NODES))
                line16 = jnp.broadcast_to(line & (NODES - 1), (16, LANES)).astype(jnp.int16)
                hots.append(
                    jnp.concatenate(
                        [hot(line16 == iota_c[k * 16 : k * 16 + 16, :]) for k in range(NODES // 16)],
                        axis=0,
                    )
                )
            away = value * jnp.concatenate(far, axis=0)
            f2[...] += mm(
                jnp.concatenate(hots, axis=1), jnp.concatenate([value - away, away], axis=1)
            )

    def total_of(ref):
        total = ref[0].astype(F32)
        for i in range(1, 4):
            total = total + ref[i].astype(F32)
        return total.astype(BF16)

    stage = [send(0, wg_ref.at[half_rows(1 - core), :], pair, partner)]
    started = list(stage)
    stage[0].start()
    scatter(0, 2)
    stage[0].wait_recv()
    half[...] = (wg_ref[half_rows(core), :].astype(F32) + pair[...].astype(F32)).astype(BF16)
    stage = [
        send(i, half.at[quarter_rows(to), :], quarter.at[i], device)
        for i, (to, device) in enumerate(y_peers, 1)
    ]
    for c in stage:
        c.start()
    started += stage
    scatter(2, 5)
    for c in stage:
        c.wait_recv()
    quarter[0] = half[quarter_rows(y), :]
    part[...] = total_of(quarter)
    stage = [send(i, part, along_z.at[z], device) for i, device in enumerate(z_peers, 4)]
    for c in stage:
        c.start()
    started += stage
    along_z[z] = part[...]
    scatter(5, 8)
    for c in stage:
        c.wait_recv()
    other[...] = total_of(along_z)
    stage = [send(i, other, along_x.at[x], device) for i, device in enumerate(x_peers, 7)]
    for c in stage:
        c.start()
    started += stage
    along_x[x] = other[...]
    scatter(8, 11)
    for c in stage:
        c.wait_recv()
    third[mine(), :] = total_of(along_x)
    stage = [
        send(i, third.at[mine(), :], third.at[mine(), :], device)
        for i, (_, device) in enumerate(y_peers, 10)
    ]
    for c in stage:
        c.start()
    started += stage
    scatter(11, BLOCKS)

    w_s = ewi_ref[D : 2 * D]
    border[...] = mm_t(f2[:, D : 2 * D].astype(BF16), w_s).astype(BF16)
    for j in range(4):
        start(j)
    for c in stage:
        c.wait_recv()
    stage = [send(13, third.at[half_rows(core), :], third.at[half_rows(core), :], partner)]
    stage[0].start()
    started += stage
    near = mm_t(f2[:, 0:D].astype(BF16), w_s)
    for j in range(4):
        finish(j)
    hots = []
    for j in range(4):
        for c in range(HALO // LANES):
            line = out_rows_ref[j : j + 1, c * LANES : (c + 1) * LANES]
            line16 = jnp.broadcast_to(line, (16, LANES)).astype(jnp.int16)
            hots.append(
                jnp.concatenate(
                    [hot(line16 == iota_c[k * 16 : k * 16 + 16, :]) for k in range(NODES // 16)],
                    axis=0,
                )
            )
    node_ref[...] = own_ref[...] + near + mm(jnp.concatenate(hots, axis=1), landing[...])
    stage[0].wait_recv()
    sum_ref[...] = third[...]
    for c in started:
        c.wait_send()


def scatter_call(wide, narrow, first, send, own, wg, ewi, out_rows):
    vm = pl.BlockSpec(memory_space=pltpu.VMEM)
    v = pltpu.VMEM
    sem = pltpu.SemaphoreType.DMA
    quarter = W_ROWS // 8
    return pl.pallas_call(
        functools.partial(scatter_kernel, wide, narrow),
        out_shape=(
            jax.ShapeDtypeStruct((NODES, D), F32),
            jax.ShapeDtypeStruct((W_ROWS, D), BF16),
        ),
        in_specs=[pl.BlockSpec(memory_space=pl.ANY)] + [vm] * 5,
        out_specs=(vm, vm),
        scratch_shapes=[
            v((EDGES, D), BF16), v((NODES, 2 * D), F32), v((NODES, LANES), jnp.int16),
            v((4 * HALO, D), BF16), v((4 * HALO, D), BF16),
            v((W_ROWS // 2, D), BF16), v((W_ROWS // 2, D), BF16), v((4, quarter, D), BF16),
            v((quarter, D), BF16), v((4, quarter, D), BF16), v((quarter, D), BF16),
            v((4, quarter, D), BF16), v((W_ROWS, D), BF16),
            sem((BLOCKS,)), sem((4,)), sem((4,)), sem((14,)), sem((14,)),
        ],
        compiler_params=pltpu.CompilerParams(
            collective_id=1, has_side_effects=True, vmem_limit_bytes=VMEM_LIMIT
        ),
        name="scatter",
    )(first, send, own, wg, ewi, out_rows)


def unpack_kernel(scales, sum_ref, *outs):
    at = 0
    for out, scale in zip(outs, scales):
        rows = out.shape[0]
        out[...] = sum_ref[at : at + rows, :].astype(F32) * scale
        at += rows


def unpack_call(scales, summed, shapes):
    vm = pl.BlockSpec(memory_space=pltpu.VMEM)
    return pl.pallas_call(
        functools.partial(unpack_kernel, scales),
        out_shape=tuple(jax.ShapeDtypeStruct(s, F32) for s in shapes),
        in_specs=[vm],
        out_specs=(vm,) * 6,
        name="unpack",
    )(summed)


def per_device(
    wide,
    narrow,
    node_hidden_state,
    edge_hidden_state,
    node_output_gradient,
    edge_output_gradient,
    senders,
    receivers,
    edge_slot_count,
    outbound_rows,
    *weights,
):
    out_rows = outbound_rows.reshape(4, HALO)
    send = senders.reshape(EDGES // LANES, LANES)
    recv = receivers.reshape(EDGES // LANES, LANES)
    picked = gather_call(wide, narrow, node_hidden_state, out_rows, send)
    edge_grad, first, own, wg = partition_call(
        edge_slot_count,
        node_hidden_state,
        node_output_gradient,
        edge_hidden_state,
        edge_output_gradient,
        picked,
        recv,
        weights,
    )
    node_grad, summed = scatter_call(wide, narrow, first, send, own, wg, weights[0], out_rows)
    edge_scale = 1.0 / math.sqrt(EDGES * wide * narrow)
    node_scale = 1.0 / math.sqrt(NODES * wide * narrow)
    sums = unpack_call((edge_scale,) * 3 + (node_scale,) * 3, summed, [x.shape for x in weights])
    return (node_grad, edge_grad, *sums)


def solution(mesh):
    both = ("wide", "narrow")
    rows, flat = P(both, None), P(both)
    return jax.shard_map(
        functools.partial(per_device, mesh.shape["wide"], mesh.shape["narrow"]),
        mesh=mesh,
        in_specs=(rows, rows, rows, rows, flat, flat, flat, P(both, None, None)) + (P(),) * 6,
        out_specs=(rows, rows) + (P(),) * 6,
        check_vma=False,
    )
```

time: 152 us -> 119 us (0.78)
  Pallas kernels: 148 us -> 114 us
  local copies, waits for them, and re-layouts: 0 us -> 2.26 us
    pallas_call x1, Pallas kernels: 64.1 us -> 45.1 us  [partition_call(): pl.pallas_call(partition_kernel, out_shape=(jax.ShapeDtypeStruct((EDGES,...]
    pallas_call x3, Pallas kernels: 84.4 us -> 68.8 us  [the longest x1 38.5 us: scatter_call(): pl.pallas_call(functools.partial(scatter_kernel, wide, narrow), out_shape...]
    unnamed x0 -> x1, local copies, waits for them, and re-layouts: none -> 2.26 us
where the time goes in v2:
time: 119 us; the launch traced here: 117 us
  Pallas kernels  114 us (96%)
  local copies, waits for them, and re-layouts  2.26 us (2%)
  between operations  1.3 us (1%)
    pallas_call x1, Pallas kernels, partition_call(): pl.pallas_call(partition_kernel, out_shape=(jax.ShapeDtypeStruct((EDGES,...  45.1 us
    pallas_call x1, Pallas kernels, scatter_call(): pl.pallas_call(functools.partial(scatter_kernel, wide, narrow), out_shape...  38.5 us
    pallas_call x1, Pallas kernels, gather_call(): pl.pallas_call(functools.partial(gather_kernel, wide, narrow), out_shape=...  28.5 us

profile of v2, /device:TPU:32, one launch (start us, length us, event | category | flops | bytes accessed | tf_op | source)
XLA Modules:
  0.0 117.5 jit_solution(16280388145296671739)
XLA Ops:
  1.3 28.5 %gather.1.picked_hbm = bf16[12288,128]{1,0:T(8,128)(2,1)} custom-call(bf16[2048,128]{1,0:T(8,128)(2,1)} %node_ref.3, s32[4,512]{1,0:T(4,128)} %bitcast.7, s32[96,128]{1,0:T(8,128)} %bitcast.5), custom_call_target="tpu_custom_call" | custom-call | tf_op jit(solution)/shard_map/gather/pallas_call | solution.py:486
  29.8 45.1 %partition.1 = (bf16[12288,128]{1,0:T(8,128)(2,1)}, bf16[12288,128]{1,0:T(8,128)(2,1)}, f32[2048,128]{1,0:T(8,128)}, bf16[1280,128]{1,0:T(8,128)(2,1)}) custom-call(s32[1]{0:T(128)S(6)} %copy.23.count_ref, s32[96,128]{1,0:T(8,128)} %bitcast.3, bf16[2048,128]{1,0:T(8,128)(2,1)} %node_ref.3, bf16[2048,128]{1,0:T(8,128)(2,1)} %ncot_ref.1, ...), custom_call_target="tpu_custom_call" | custom-call | tf_op jit(solution)/shard_map/partition/pallas_call | solution.py:336
  74.9 38.5 %scatter.1 = (f32[2048,128]{1,0:T(8,128)}, bf16[1280,128]{1,0:T(8,128)(2,1)}) custom-call(bf16[12288,128]{1,0:T(8,128)(2,1)} %get-tuple-element.20.first_hbm, s32[96,128]{1,0:T(8,128)} %bitcast.6, f32[2048,128]{1,0:T(8,128)} %get-tuple-element.21.own_ref, bf16[1280,128]{1,0:T(8,128)(2,1)} %get-tuple-element.22.wg_ref, bf16[384,128]{1,0:T(8,128)(2,1)} %ewi_ref.3, ...), custom_call_target="tpu_custom_call" | custom-call | tf_op jit(solution)/shard_map/scatter/pallas_call | solution.py:667
  113.4 1.8 %unpack.1 = (f32[384,128]{1,0:T(8,128)}, f32[128,128]{1,0:T(8,128)}, f32[128,128]{1,0:T(8,128)}, f32[256,128]{1,0:T(8,128)}, f32[128,128]{1,0:T(8,128)}, /*index=5*/f32[128,128]{1,0:T(8,128)}) custom-call(bf16[1280,128]{1,0:T(8,128)(2,1)} %get-tuple-element.25.sum_ref), custom_call_target="tpu_custom_call" | custom-call | tf_op jit(solution)/shard_map/unpack/pallas_call | solution.py:700
  115.2 2.3 %copy.24 = f32[2048,128]{1,0:T(8,128)} copy(f32[2048,128]{1,0:T(8,128)} %get-tuple-element.40) | data formatting | bytes 2097152

commit v3 on v2

--- a/solution.py
+++ b/solution.py
@@ -27,7 +27,10 @@
 ROWS = BLOCK // LANES
 PADDED = NODES + WINDOW
 W_ROWS = 1280
-EARLY = 4
+STEP = 2048
+STEPS = EDGES // STEP
+STEP_ROWS = STEP // LANES
+EARLY = 6
 VMEM_LIMIT = 62 * 1024 * 1024
 
 
@@ -49,8 +52,12 @@
     return a.astype(BF16), (s + a * (1.0 - s)).astype(BF16)
 
 
-def normalise(top):
-    centred = top - jnp.mean(top, axis=-1, keepdims=True)
+def centre_columns(weight):
+    wide = weight.astype(F32)
+    return (wide - jnp.mean(wide, axis=-1, keepdims=True)).astype(BF16)
+
+
+def normalise(centred):
     inverse = lax.rsqrt(jnp.mean(centred * centred, axis=-1, keepdims=True) + EPS)
     return centred * inverse, inverse
 
@@ -101,6 +108,7 @@
     def _(b):
         block_copy(cot_hbm, cot_v, sem_c, b).start()
 
+    ewo_c, nwo_c = centre_columns(ewo_ref[...]), centre_columns(nwo_ref[...])
     w_e, w_es, w_r = ewi_ref[0:D], ewi_ref[0 : 2 * D], ewi_ref[2 * D : 3 * D]
 
     for i in range(NODES // NODE_CHUNK):
@@ -185,7 +193,7 @@
             act2, slope2 = silu_pair(mm(act1, ewm_ref[...]))
             a2[at, :] = act2
             d2[at, :] = slope2
-            normed, inverse = normalise(mm(act2, ewo_ref[...]))
+            normed, inverse = normalise(mm(act2, ewo_c))
             nrm[at, :] = normed.astype(BF16)
             inv[at, :] = jnp.broadcast_to(inverse, (CHUNK, D)).astype(BF16)
         rows = pl.ds(b * BLOCK, BLOCK)
@@ -224,7 +232,7 @@
         inputs = jnp.concatenate([own, total], axis=1)
         act1, slope1 = silu_pair(mm(inputs, nwi_ref[...]))
         act2, slope2 = silu_pair(mm(act1, nwm_ref[...]))
-        normed, inverse = normalise(mm(act2, nwo_ref[...]))
+        normed, inverse = normalise(mm(act2, nwo_c))
         g = ncot_ref[at, :].astype(F32)
         top = norm_grad(g, normed, inverse).astype(BF16)
         wno[...] += t_mm(act2, top)
@@ -421,10 +429,10 @@
     greet, start, finish = swap_halos(w, v, wide, narrow, outgoing, landing, send_sem, recv_sem)
     barrier = pltpu.get_barrier_semaphore()
     peers = greet(barrier)
-    iota_ref[...] = lax.broadcasted_iota(jnp.int32, (LANES, NODES), 1).astype(jnp.int16)
     half = NODES // 2
-    table[0:half, 0:D] = node_ref[0:half, :]
-    table[0:half, D : 2 * D] = node_ref[half:NODES, :]
+    iota_ref[...] = lax.broadcasted_iota(jnp.int32, (LANES, half), 1).astype(jnp.int16)
+    table[:, 0:D] = node_ref[0:half, :]
+    table[:, D : 2 * D] = node_ref[half:NODES, :]
 
     for j in range(4):
         hots, high = [], []
@@ -432,7 +440,7 @@
             col = columns_of(out_rows_ref[j : j + 1, c * LANES : (c + 1) * LANES])
             high.append(col >= half)
             hots.append(column_hot((col & (half - 1)).astype(jnp.int16), iota_ref, half))
-        both = mm(jnp.concatenate(hots, axis=0), table[0:half, :])
+        both = mm(jnp.concatenate(hots, axis=0), table[:, 0 : 2 * D])
         rows = jnp.where(jnp.concatenate(high, axis=0), both[:, D:], both[:, :D])
         outgoing[pl.ds(j * HALO, HALO), :] = rows.astype(BF16)
         if j == 0:
@@ -440,42 +448,47 @@
         start(j)
 
     def out_copy(b):
-        at = pl.ds(b * BLOCK, BLOCK)
+        at = pl.ds(b * STEP, STEP)
         return pltpu.make_async_copy(held.at[at, :], picked_hbm.at[at, :], out_sem.at[b])
 
     def pick(b, own, far):
-        hots, high = [], []
-        for r in range(ROWS):
-            col = columns_of(send_ref[pl.ds(b * ROWS + r, 1), :])
+        hots, high, halo = [], [], []
+        for r in range(STEP_ROWS):
+            col = columns_of(send_ref[pl.ds(b * STEP_ROWS + r, 1), :])
             high.append((col & half) != 0)
-            place = (col & (half - 1)) + jnp.where(col >= NODES, half, 0)
-            if not own:
-                place = place - half
-            hots.append(column_hot(place.astype(jnp.int16), iota_ref, half * (own + far)))
-        lower = 0 if own else half
-        both = mm(jnp.concatenate(hots, axis=0), table[lower : lower + half * (own + far), :])
-        return jnp.where(jnp.concatenate(high, axis=0), both[:, D:], both[:, :D]).astype(BF16)
+            halo.append(col >= NODES)
+            hots.append(column_hot((col & (half - 1)).astype(jnp.int16), iota_ref, half))
+        upper, away = jnp.concatenate(high, axis=0), jnp.concatenate(halo, axis=0)
+        lanes = slice(0 if own else 2 * D, 4 * D if far else 2 * D)
+        found = mm(jnp.concatenate(hots, axis=0), table[:, lanes])
+
+        def side(at):
+            return jnp.where(upper, found[:, at + D : at + 2 * D], found[:, at : at + D])
+
+        near_rows = side(0) if own else 0.0
+        far_rows = side(2 * D if own else 0) if far else 0.0
+        return jnp.where(away, far_rows, near_rows).astype(BF16)
 
     @pl.loop(0, EARLY)
     def _(b):
-        held[pl.ds(b * BLOCK, BLOCK), :] = pick(b, True, False)
+        held[pl.ds(b * STEP, STEP), :] = pick(b, True, False)
 
     for j in range(4):
         finish(j)
-    table[half:NODES, 0:D] = landing[0:half, :]
-    table[half:NODES, D : 2 * D] = landing[half:NODES, :]
+    table[:, 2 * D : 3 * D] = landing[0:half, :]
+    table[:, 3 * D : 4 * D] = landing[half:NODES, :]
 
     @pl.loop(0, EARLY)
     def _(b):
-        held[pl.ds(b * BLOCK, BLOCK), :] += pick(b, False, True)
+        held[pl.ds(b * STEP, STEP), :] += pick(b, False, True)
         out_copy(b).start()
 
-    @pl.loop(EARLY, BLOCKS)
-    def _(b):
-        held[pl.ds(b * BLOCK, BLOCK), :] = pick(b, True, True)
+    @pl.loop(EARLY, STEPS)
+    def _(b):
+        held[pl.ds(b * STEP, STEP), :] = pick(b, True, True)
         out_copy(b).start()
 
-    @pl.loop(0, BLOCKS)
+    @pl.loop(0, STEPS)
     def _(b):
         out_copy(b).wait()
 
@@ -491,10 +504,10 @@
         scratch_shapes=[
             pltpu.VMEM((4 * HALO, D), BF16),
             pltpu.VMEM((4 * HALO, D), BF16),
-            pltpu.VMEM((NODES, 2 * D), BF16),
-            pltpu.VMEM((LANES, NODES), jnp.int16),
+            pltpu.VMEM((NODES // 2, 4 * D), BF16),
+            pltpu.VMEM((LANES, NODES // 2), jnp.int16),
             pltpu.VMEM((EDGES, D), BF16),
-            sem((4,)), sem((4,)), sem((BLOCKS,)),
+            sem((4,)), sem((4,)), sem((STEPS,)),
         ],
         compiler_params=pltpu.CompilerParams(
             collective_id=0, has_side_effects=True, vmem_limit_bytes=VMEM_LIMIT
@@ -515,10 +528,10 @@
     n_half, n_quarter = W_ROWS // 2, W_ROWS // 8
 
     def block_copy(b):
-        at = pl.ds(b * BLOCK, BLOCK)
+        at = pl.ds(b * STEP, STEP)
         return pltpu.make_async_copy(first_hbm.at[at, :], first_v.at[at, :], first_sem.at[b])
 
-    @pl.loop(0, BLOCKS)
+    @pl.loop(0, STEPS)
     def _(b):
         block_copy(b).start()
 
@@ -539,7 +552,6 @@
 
     iota_c[...] = lax.broadcasted_iota(jnp.int32, (NODES, LANES), 0).astype(jnp.int16)
     f2[...] = jnp.zeros_like(f2)
-    pl.semaphore_wait(barrier, peers + len(others))
 
     def send(i, src, dst, device):
         return pltpu.make_async_remote_copy(
@@ -556,27 +568,35 @@
     def mine():
         return pl.ds(pl.multiple_of(core * n_half + y * n_quarter, 16), n_quarter)
 
-    def scatter(lo, hi):
+    def scatter(far, lo, hi):
+        into = pl.ds(HALO if far else 0, HALO)
+
         @pl.loop(lo, hi)
         def _(b):
-            block_copy(b).wait()
-            rows = pl.ds(b * BLOCK, BLOCK)
-            value = first_v[rows, :]
-            far, hots = [], []
-            for r in range(ROWS):
-                line = send_ref[pl.ds(b * ROWS + r, 1), :]
-                far.append(hot(columns_of(line) >= NODES))
-                line16 = jnp.broadcast_to(line & (NODES - 1), (16, LANES)).astype(jnp.int16)
-                hots.append(
+            if far:
+                block_copy(b).wait()
+            parts, hots = [], []
+            for r in range(STEP_ROWS):
+                line = send_ref[pl.ds(b * STEP_ROWS + r, 1), :]
+                value = first_v[pl.ds(b * STEP + r * LANES, LANES), :]
+                group = (columns_of(line) // HALO).astype(jnp.int16)
+                parts.append(
                     jnp.concatenate(
-                        [hot(line16 == iota_c[k * 16 : k * 16 + 16, :]) for k in range(NODES // 16)],
-                        axis=0,
+                        [
+                            jnp.where(group == jnp.int16(4 * far + j), value, jnp.zeros((), BF16))
+                            for j in range(4)
+                        ],
+                        axis=1,
                     )
                 )
-            away = value * jnp.concatenate(far, axis=0)
-            f2[...] += mm(
-                jnp.concatenate(hots, axis=1), jnp.concatenate([value - away, away], axis=1)
-            )
+                hots.append(row_hot(line & (HALO - 1), HALO))
+            f2[into, :] += mm(jnp.concatenate(hots, axis=1), jnp.concatenate(parts, axis=0))
+
+    def row_hot(line, height):
+        line16 = jnp.broadcast_to(line, (16, LANES)).astype(jnp.int16)
+        return jnp.concatenate(
+            [hot(line16 == iota_c[k * 16 : k * 16 + 16, :]) for k in range(height // 16)], axis=0
+        )
 
     def total_of(ref):
         total = ref[0].astype(F32)
@@ -584,10 +604,21 @@
             total = total + ref[i].astype(F32)
         return total.astype(BF16)
 
+    w_s = ewi_ref[D : 2 * D]
+
+    def send_border():
+        for j in range(4):
+            border[j * HALO : (j + 1) * HALO, :] = mm_t(
+                f2[HALO : 2 * HALO, j * D : (j + 1) * D].astype(BF16), w_s
+            ).astype(BF16)
+            start(j)
+
+    scatter(True, 0, 1)
+    pl.semaphore_wait(barrier, peers + len(others))
     stage = [send(0, wg_ref.at[half_rows(1 - core), :], pair, partner)]
     started = list(stage)
     stage[0].start()
-    scatter(0, 2)
+    scatter(True, 1, 2)
     stage[0].wait_recv()
     half[...] = (wg_ref[half_rows(core), :].astype(F32) + pair[...].astype(F32)).astype(BF16)
     stage = [
@@ -597,7 +628,7 @@
     for c in stage:
         c.start()
     started += stage
-    scatter(2, 5)
+    scatter(True, 2, 4)
     for c in stage:
         c.wait_recv()
     quarter[0] = half[quarter_rows(y), :]
@@ -607,7 +638,8 @@
         c.start()
     started += stage
     along_z[z] = part[...]
-    scatter(5, 8)
+    scatter(True, 4, STEPS)
+    send_border()
     for c in stage:
         c.wait_recv()
     other[...] = total_of(along_z)
@@ -616,7 +648,7 @@
         c.start()
     started += stage
     along_x[x] = other[...]
-    scatter(8, 11)
+    scatter(False, 0, 2)
     for c in stage:
         c.wait_recv()
     third[mine(), :] = total_of(along_x)
@@ -627,32 +659,26 @@
     for c in stage:
         c.start()
     started += stage
-    scatter(11, BLOCKS)
-
-    w_s = ewi_ref[D : 2 * D]
-    border[...] = mm_t(f2[:, D : 2 * D].astype(BF16), w_s).astype(BF16)
-    for j in range(4):
-        start(j)
+    scatter(False, 2, 4)
+
     for c in stage:
         c.wait_recv()
     stage = [send(13, third.at[half_rows(core), :], third.at[half_rows(core), :], partner)]
     stage[0].start()
     started += stage
-    near = mm_t(f2[:, 0:D].astype(BF16), w_s)
+    scatter(False, 4, STEPS)
+    for j in range(4):
+        rows = slice(j * HALO, (j + 1) * HALO)
+        near = f2[0:HALO, j * D : (j + 1) * D].astype(BF16)
+        node_ref[rows, :] = own_ref[rows, :] + mm_t(near, w_s)
+    hots = [
+        row_hot(out_rows_ref[j : j + 1, c * LANES : (c + 1) * LANES], NODES)
+        for j in range(4)
+        for c in range(HALO // LANES)
+    ]
     for j in range(4):
         finish(j)
-    hots = []
-    for j in range(4):
-        for c in range(HALO // LANES):
-            line = out_rows_ref[j : j + 1, c * LANES : (c + 1) * LANES]
-            line16 = jnp.broadcast_to(line, (16, LANES)).astype(jnp.int16)
-            hots.append(
-                jnp.concatenate(
-                    [hot(line16 == iota_c[k * 16 : k * 16 + 16, :]) for k in range(NODES // 16)],
-                    axis=0,
-                )
-            )
-    node_ref[...] = own_ref[...] + near + mm(jnp.concatenate(hots, axis=1), landing[...])
+    node_ref[...] += mm(jnp.concatenate(hots, axis=1), landing[...])
     stage[0].wait_recv()
     sum_ref[...] = third[...]
     for c in started:
@@ -673,12 +699,12 @@
         in_specs=[pl.BlockSpec(memory_space=pl.ANY)] + [vm] * 5,
         out_specs=(vm, vm),
         scratch_shapes=[
-            v((EDGES, D), BF16), v((NODES, 2 * D), F32), v((NODES, LANES), jnp.int16),
+            v((EDGES, D), BF16), v((2 * HALO, 4 * D), F32), v((NODES, LANES), jnp.int16),
             v((4 * HALO, D), BF16), v((4 * HALO, D), BF16),
             v((W_ROWS // 2, D), BF16), v((W_ROWS // 2, D), BF16), v((4, quarter, D), BF16),
             v((quarter, D), BF16), v((4, quarter, D), BF16), v((quarter, D), BF16),
             v((4, quarter, D), BF16), v((W_ROWS, D), BF16),
-            sem((BLOCKS,)), sem((4,)), sem((4,)), sem((14,)), sem((14,)),
+            sem((STEPS,)), sem((4,)), sem((4,)), sem((14,)), sem((14,)),
         ],
         compiler_params=pltpu.CompilerParams(
             collective_id=1, has_side_effects=True, vmem_limit_bytes=VMEM_LIMIT
@@ -687,23 +713,31 @@
     )(first, send, own, wg, ewi, out_rows)
 
 
-def unpack_kernel(scales, sum_ref, *outs):
+def unpack_kernel(scales, node_ref, sum_ref, node_out, *rest):
+    *outs, sem = rest
+    copy = pltpu.make_async_copy(node_ref, node_out, sem)
+    copy.start()
     at = 0
     for out, scale in zip(outs, scales):
         rows = out.shape[0]
         out[...] = sum_ref[at : at + rows, :].astype(F32) * scale
         at += rows
-
-
-def unpack_call(scales, summed, shapes):
+    copy.wait()
+
+
+def unpack_call(scales, node, summed, shapes):
     vm = pl.BlockSpec(memory_space=pltpu.VMEM)
+    hb = pl.BlockSpec(memory_space=pl.ANY)
     return pl.pallas_call(
         functools.partial(unpack_kernel, scales),
-        out_shape=tuple(jax.ShapeDtypeStruct(s, F32) for s in shapes),
-        in_specs=[vm],
-        out_specs=(vm,) * 6,
+        out_shape=(jax.ShapeDtypeStruct((NODES, D), F32),)
+        + tuple(jax.ShapeDtypeStruct(s, F32) for s in shapes),
+        in_specs=[vm, vm],
+        out_specs=(hb,) + (vm,) * 6,
+        scratch_shapes=[pltpu.SemaphoreType.DMA(())],
+        compiler_params=pltpu.CompilerParams(vmem_limit_bytes=VMEM_LIMIT),
         name="unpack",
-    )(summed)
+    )(node, summed)
 
 
 def per_device(
@@ -736,7 +770,9 @@
     node_grad, summed = scatter_call(wide, narrow, first, send, own, wg, weights[0], out_rows)
     edge_scale = 1.0 / math.sqrt(EDGES * wide * narrow)
     node_scale = 1.0 / math.sqrt(NODES * wide * narrow)
-    sums = unpack_call((edge_scale,) * 3 + (node_scale,) * 3, summed, [x.shape for x in weights])
+    node_grad, *sums = unpack_call(
+        (edge_scale,) * 3 + (node_scale,) * 3, node_grad, summed, [x.shape for x in weights]
+    )
     return (node_grad, edge_grad, *sums)
 
 

time: 119 us -> 105 us (0.88); the launches traced: 117 us -> 105 us
  Pallas kernels: 114 us -> 103 us
  local copies, waits for them, and re-layouts: 2.26 us -> 0 us
    pallas_call x1, Pallas kernels: 45.1 us -> 34 us  [partition_call(): pl.pallas_call(partition_kernel, out_shape=(jax.ShapeDtypeStruct((EDGES,...]
    pallas_call x1, Pallas kernels: 28.5 us -> 22.8 us  [gather_call(): pl.pallas_call(functools.partial(gather_kernel, wide, narrow), out_shape=...]
    pallas_call x1, Pallas kernels: 38.5 us -> 43.6 us  [scatter_call(): pl.pallas_call(functools.partial(scatter_kernel, wide, narrow), out_shape...]
    unnamed x1 -> x0, local copies, waits for them, and re-layouts: 2.26 us -> none
    pallas_call x1, Pallas kernels: 1.78 us -> 3.07 us  [unpack_call(): pl.pallas_call(functools.partial(unpack_kernel, scales), out_shape=(jax.S...]
where the time goes in v3:
time: 105 us
  Pallas kernels  103 us (98%)
  between operations  1.48 us (1%)
    pallas_call x1, Pallas kernels, scatter_call(): pl.pallas_call(functools.partial(scatter_kernel, wide, narrow), out_shape...  43.6 us
    pallas_call x1, Pallas kernels, partition_call(): pl.pallas_call(partition_kernel, out_shape=(jax.ShapeDtypeStruct((EDGES,...  34 us
    pallas_call x1, Pallas kernels, gather_call(): pl.pallas_call(functools.partial(gather_kernel, wide, narrow), out_shape=...  22.8 us
    pallas_call x1, Pallas kernels, unpack_call(): pl.pallas_call(functools.partial(unpack_kernel, scales), out_shape=(jax.S...  3.07 us

profile of v3, /device:TPU:32, one launch (start us, length us, event | category | flops | bytes accessed | tf_op | source)
XLA Modules:
  0.0 105.0 jit_solution(11606699770584181775)
XLA Ops:
  1.3 22.8 %gather.1.picked_hbm = bf16[12288,128]{1,0:T(8,128)(2,1)} custom-call(bf16[2048,128]{1,0:T(8,128)(2,1)} %node_ref.3, s32[4,512]{1,0:T(4,128)} %bitcast.7, s32[96,128]{1,0:T(8,128)} %bitcast.5), custom_call_target="tpu_custom_call" | custom-call | tf_op jit(solution)/shard_map/gather/pallas_call | solution.py:499
  24.1 34.0 %partition.1 = (bf16[12288,128]{1,0:T(8,128)(2,1)}, bf16[12288,128]{1,0:T(8,128)(2,1)}, f32[2048,128]{1,0:T(8,128)}, bf16[1280,128]{1,0:T(8,128)(2,1)}) custom-call(s32[1]{0:T(128)S(6)} %copy.22.count_ref, s32[96,128]{1,0:T(8,128)} %bitcast.3, bf16[2048,128]{1,0:T(8,128)(2,1)} %node_ref.3, bf16[2048,128]{1,0:T(8,128)(2,1)} %ncot_ref.1, ...), custom_call_target="tpu_custom_call" | custom-call | tf_op jit(solution)/shard_map/partition/pallas_call | solution.py:344
  58.1 43.6 %scatter.1 = (f32[2048,128]{1,0:T(8,128)}, bf16[1280,128]{1,0:T(8,128)(2,1)}) custom-call(bf16[12288,128]{1,0:T(8,128)(2,1)} %get-tuple-element.21.first_hbm, s32[96,128]{1,0:T(8,128)} %bitcast.6, f32[2048,128]{1,0:T(8,128)} %get-tuple-element.22.own_ref, bf16[1280,128]{1,0:T(8,128)(2,1)} %get-tuple-element.23.wg_ref, bf16[384,128]{1,0:T(8,128)(2,1)} %ewi_ref.3, ...), custom_call_target="tpu_custom_call" | custom-call | tf_op jit(solution)/shard_map/scatter/pallas_call | solution.py:693
  101.7 3.1 %unpack.1 = (f32[2048,128]{1,0:T(8,128)}, f32[384,128]{1,0:T(8,128)}, f32[128,128]{1,0:T(8,128)}, f32[128,128]{1,0:T(8,128)}, f32[256,128]{1,0:T(8,128)}, /*index=5*/f32[128,128]{1,0:T(8,128)}, f32[128,128]{1,0:T(8,128)}) custom-call(f32[2048,128]{1,0:T(8,128)} %get-tuple-element.24.node_ref, bf16[1280,128]{1,0:T(8,128)(2,1)} %get-tuple-element.25.sum_ref), custom_call_target="tpu_custom_call" | custom-call | tf_op jit(solution)/shard_map/unpack/pallas_call | solution.py:731
